TPU v7x, 128 devices: a whole 4x4x4 slice. The times are simulated.
128 devices in a mesh: instance: 4 (over x), layout: 4 (over y), tensor: 8 (over z, core).
Axes of the slice: x: 4, y: 4, z: 4, core: 2. Of those that a mesh axis runs over, the one named last changes fastest.
Arguments:
- prefill_pool: bfloat16 [4608, 2, 8, 64, 128], P(('instance', 'layout', 'tensor')), may hold values from -6 to 6
- lengths: int32 [16], replicated, may hold values from 10240 to 32768, as said below
- src_table: int32 [16, 512], replicated, may hold values from 0 to 4607, as said below
- dst_table: int32 [16, 512], replicated, may hold values from 0 to 4607, as said below
- row_request: int32 [64], replicated, may hold values from 0 to 15, as said below
- positions: int32 [64], replicated, may hold values from 1 to 32768, as said below
- queries: bfloat16 [4, 64, 16384], P(None, 'instance', 'tensor'), may hold values from -80 to 80
- step_key_value: bfloat16 [4, 64, 2, 8, 128], P(None, 'instance', None, 'tensor'), may hold values from -6 to 6
- out_weight: bfloat16 [16384, 16384], P('tensor', ('instance', 'layout')), may hold values from -0.046875 to 0.046875
- residual: bfloat16 [4, 64, 16384], P(None, None, ('instance', 'layout', 'tensor')), may hold values from -4 to 4
Outputs:
- decode_pool: bfloat16 [4608, 2, 8, 64, 128], P(('instance', 'layout'), None, 'tensor')
- attn_out: float32 [4, 64, 16384], P(None, None, ('instance', 'layout', 'tensor'))
Inputs may be any that keep to these rules, and one draw needn't show every extreme that they name: `lengths`: exactly one request has 32768 tokens; every other has at most 12288. `src_table`: each request r is prefilled by one instance group p(r): its live pages name distinct rows of prefill_pool, page j on the device of group p(r) with layout index j mod 4 and tensor index (j // 4) mod 8; so one device holds at most 16 live pages of one request. Entries of pages that are not live name some row of group p(r). The pairs (p(r), g(r)) with g(r) of dst_table are all distinct. `dst_table`: each request r is decoded by one instance group g(r): its live pages name distinct rows of decode_pool on the devices of that group, page j on layout index j mod 4. Entries of pages that are not live name some row of group g(r). `row_request`: the rows of instance index i (rows i * 16 onward) belong to the requests that group i decodes, 4 rows each. `positions`: at most the length of the row's request; one row of every request sees its whole prompt.
All inputs are finite; a program needn't handle non-finite values.
Results may differ from a plain program's by a relative error of at most 0.00305.
Values may be sent and summed in bfloat16 or wider, within the bound.
A program may use at most 128 MiB of HBM per device.

v0:
```python
import jax
import jax.numpy as jnp
from jax import lax
from jax.sharding import PartitionSpec as P

OTHERLEN = 12288


def joined(value, axis, join):
    pieces = jax.tree.map(lambda part: lax.all_gather(part, axis), value)
    head = jax.tree.map(lambda part: part[0], pieces)
    tail = jax.tree.map(lambda part: part[1:], pieces)
    total, _ = lax.scan(lambda total, piece: (join(total, piece), None), head, tail)
    return total


def join_stats(first, second):
    top = jnp.maximum(first[0], second[0])
    left = jnp.exp(first[0] - top)
    right = jnp.exp(second[0] - top)
    total = first[1] * left + second[1] * right
    weighted = first[2] * left[..., None] + second[2] * right[..., None]
    return (top, total, weighted)


def shards(
    prefill_pool,
    lengths,
    src_table,
    dst_table,
    row_request,
    positions,
    queries,
    step_key_value,
    out_weight,
    residual,
):
    n_inst = lax.axis_size("instance")
    n_lay = lax.axis_size("layout")
    n_ten = lax.axis_size("tensor")
    inst = lax.axis_index("instance")
    lay = lax.axis_index("layout")
    ten = lax.axis_index("tensor")
    src_dev = prefill_pool.shape[0]
    heads_kv = prefill_pool.shape[2]
    page = prefill_pool.shape[3]
    head_dim = prefill_pool.shape[4]
    requests, max_pages = src_table.shape
    kv_local = heads_kv // n_ten
    slot_count = max_pages // n_lay + (n_inst - 1) * (OTHERLEN // page // n_lay) + 16
    spread = n_lay * n_ten
    capacity = max_pages // spread
    npages = (lengths + page - 1) // page
    prod_grp = src_table[:, 0] // (src_dev * spread)
    dec_grp = dst_table[:, 0] // (slot_count * n_lay)
    groups = jnp.arange(n_inst, dtype=jnp.int32)
    req_ids = jnp.arange(requests, dtype=jnp.int32)
    steps_k = jnp.arange(capacity, dtype=jnp.int32)
    send_match = (prod_grp[None, :] == inst) & (dec_grp[None, :] == groups[:, None])
    send_req = jnp.sum(jnp.where(send_match, req_ids[None, :], 0), axis=1)
    send_page = steps_k * spread + ten * n_lay + lay
    base = ((inst * n_lay + lay) * n_ten + ten) * src_dev
    local_slot = jnp.clip(src_table[send_req[:, None], send_page[None, :]] - base, 0, src_dev - 1)
    outgoing = prefill_pool[local_slot]
    incoming = lax.all_to_all(
        lax.all_to_all(outgoing, "instance", split_axis=0, concat_axis=0, tiled=True),
        "tensor",
        split_axis=3,
        concat_axis=1,
        tiled=True,
    )
    recv_match = (prod_grp[None, :] == groups[:, None]) & (dec_grp[None, :] == inst)
    recv_req = jnp.sum(jnp.where(recv_match, req_ids[None, :], 0), axis=1)
    source_ten = jnp.arange(n_ten, dtype=jnp.int32)
    recv_page = (steps_k[None, :] * spread + source_ten[:, None] * n_lay + lay).reshape(-1)
    recv_live = recv_page[None, :] < npages[recv_req][:, None]
    target = dst_table[recv_req[:, None], recv_page[None, :]] - (inst * n_lay + lay) * slot_count
    target = jnp.where(recv_live, target, slot_count).reshape(-1)
    decode_pool = jnp.zeros((slot_count, 2, kv_local, page, head_dim), jnp.bfloat16)
    decode_pool = decode_pool.at[target].set(
        incoming.reshape(-1, 2, kv_local, page, head_dim), mode="drop"
    )
    owner_all = jnp.broadcast_to(recv_req[:, None], recv_live.shape).reshape(-1)
    page_all = jnp.broadcast_to(recv_page[None, :], recv_live.shape).reshape(-1)
    slot_req = jnp.full((slot_count,), -1, jnp.int32).at[target].set(owner_all, mode="drop")
    slot_page = jnp.zeros((slot_count,), jnp.int32).at[target].set(page_all, mode="drop")
    steps_n, group_rows, width = queries.shape
    grouped_query = width // head_dim // kv_local
    row_req = lax.dynamic_slice_in_dim(row_request, inst * group_rows, group_rows)
    row_pos = lax.dynamic_slice_in_dim(positions, inst * group_rows, group_rows)
    query_h = queries.reshape(steps_n, group_rows, kv_local, grouped_query, head_dim).transpose(
        2, 0, 1, 3, 4
    )
    query_h = query_h.reshape(kv_local, steps_n * group_rows * grouped_query, head_dim)
    n_query = steps_n * group_rows * grouped_query
    query_ids = jnp.arange(n_query, dtype=jnp.int32)
    query_row = query_ids // grouped_query % group_rows
    query_step = query_ids // (grouped_query * group_rows)
    query_req = row_req[query_row]
    query_pos = row_pos[query_row]
    scale = head_dim ** (-0.5)
    floor_val = -1e30
    fresh_k = step_key_value[:, :, 0].transpose(2, 0, 1, 3)
    fresh_v = step_key_value[:, :, 1].transpose(2, 0, 1, 3)
    fresh = (
        jnp.einsum("kqd,kurd->kqur", query_h, fresh_k, preferred_element_type=jnp.float32) * scale
    )
    fresh_ok = jnp.arange(group_rows)[None, None, :] == query_row[:, None, None]
    fresh_ok = (
        fresh_ok & (jnp.arange(steps_n)[None, :, None] <= query_step[:, None, None]) & (lay == 0)
    )
    fresh = jnp.where(fresh_ok[None], fresh, floor_val)
    start_top = jnp.max(fresh, axis=(2, 3))
    fresh_w = jnp.where(fresh_ok[None], jnp.exp(fresh - start_top[..., None, None]), 0.0)
    start_total = jnp.sum(fresh_w, axis=(2, 3))
    start_acc = jnp.einsum(
        "kqur,kurd->kqd", fresh_w.astype(jnp.bfloat16), fresh_v, preferred_element_type=jnp.float32
    )
    block = 16
    pool_k = decode_pool[:, 0]
    pool_v = decode_pool[:, 1]
    in_page = jnp.arange(page, dtype=jnp.int32)

    def visit(carry, index):
        top, total, weighted = carry
        key_blk = lax.dynamic_slice_in_dim(pool_k, index * block, block, 0)
        val_blk = lax.dynamic_slice_in_dim(pool_v, index * block, block, 0)
        req_blk = lax.dynamic_slice_in_dim(slot_req, index * block, block, 0)
        page_blk = lax.dynamic_slice_in_dim(slot_page, index * block, block, 0)
        scores = (
            jnp.einsum("kqd,bkud->kqbu", query_h, key_blk, preferred_element_type=jnp.float32)
            * scale
        )
        tokens = page_blk[:, None] * page + in_page[None, :]
        usable = (req_blk[None, :, None] == query_req[:, None, None]) & (
            tokens[None] < query_pos[:, None, None]
        )
        scores = jnp.where(usable[None], scores, floor_val)
        new_top = jnp.maximum(top, jnp.max(scores, axis=(2, 3)))
        shrink = jnp.exp(top - new_top)
        probs = jnp.where(usable[None], jnp.exp(scores - new_top[..., None, None]), 0.0)
        total = total * shrink + jnp.sum(probs, axis=(2, 3))
        weighted = weighted * shrink[..., None] + jnp.einsum(
            "kqbu,bkud->kqd",
            probs.astype(jnp.bfloat16),
            val_blk,
            preferred_element_type=jnp.float32,
        )
        return ((new_top, total, weighted), None)

    stats, unused = lax.scan(
        visit, (start_top, start_total, start_acc), jnp.arange(slot_count // block, dtype=jnp.int32)
    )
    top, total, weighted = joined(stats, "layout", join_stats)
    context = (weighted / total[..., None]).reshape(
        kv_local, steps_n, group_rows, grouped_query, head_dim
    )
    context = (
        context.transpose(1, 2, 0, 3, 4).reshape(steps_n, group_rows, width).astype(jnp.bfloat16)
    )
    projected = jnp.einsum(
        "srh,hc->src",
        lax.all_gather(context, "instance", axis=1, tiled=True),
        out_weight,
        preferred_element_type=jnp.float32,
    )
    summed = lax.psum_scatter(projected, "tensor", scatter_dimension=2, tiled=True)
    attn_out = residual.astype(jnp.float32) + summed
    return (decode_pool, attn_out)


def solution(mesh):
    in_specs = (
        P(("instance", "layout", "tensor"), None, None, None, None),
        P(),
        P(),
        P(),
        P(),
        P(),
        P(None, "instance", "tensor"),
        P(None, "instance", None, "tensor", None),
        P("tensor", ("instance", "layout")),
        P(None, None, ("instance", "layout", "tensor")),
    )
    out_specs = (
        P(("instance", "layout"), None, "tensor", None, None),
        P(None, None, ("instance", "layout", "tensor")),
    )
    return jax.shard_map(shards, mesh=mesh, in_specs=in_specs, out_specs=out_specs, check_vma=False)
```

profile of v0, /device:TPU:1, one launch (start us, length us, event | category | flops | bytes accessed | tf_op | source)
XLA Modules:
  0.0 1137.1 jit_solution(438531920745158120)
XLA Ops:
  12.6 11.3 gather_fusion.3
  23.9 8.2 copy.40
  32.1 187.4 %all_to_all.20 = bf16[4,16,2,8,64,128]{5,4,2,1,3,0:T(8,128)(2,1)S(1)} all-to-all(bf16[4,16,2,8,64,128]{5,4,2,1,3,0:T(8,128)(2,1)S(1)} %copy.40), channel_id=1, replica_groups=mesh['instance'=4,'layout'=4,'tensor'=8] {'instance'}, dimensions={0} | all-to-all | bytes 33554432 | tf_op jit(solution)/shard_map/all_to_all | solution.py:66
  219.4 6.7 copy.41
  226.2 7.6 all-to-all-start.1
  247.2 169.9 %all-to-all-done.1 = bf16[4,16,2,8,64,128]{5,4,2,1,0,3:T(8,128)(2,1)} async-done(((bf16[4,16,2,8,64,128]{5,4,2,1,0,3:T(8,128)(2,1)}), bf16[4,16,2,8,64,128]{5,4,2,1,0,3:T(8,128)(2,1)}, u32[]{:S(2)}, u32[]{:S(2)}) %all-to-all-start.1) | async-done | bytes 16777248 | tf_op jit(solution)/shard_map/all_to_all | solution.py:65
  417.1 14.3 %copy.42 = bf16[4,16,2,8,64,128]{5,4,2,1,3,0:T(8,128)(2,1)} copy(bf16[4,16,2,8,64,128]{5,4,2,1,0,3:T(8,128)(2,1)} %all-to-all-done.1) | data formatting | bytes 33554432 | tf_op jit(solution)/shard_map/all_to_all | solution.py:65
  431.4 6.2 broadcast.718
  437.6 74.4 %scatter_fusion = bf16[288,2,64,128]{3,2,1,0:T(8,128)(2,1)} fusion(bf16[288,2,64,128]{3,2,1,0:T(8,128)(2,1)} %broadcast.718, s32[512]{0:T(512)S(1)} %bitcast.204, bf16[512,2,64,128]{3,2,1,0:T(8,128)(2,1)} %bitcast.186), kind=kCustom, calls=%fused_computation.4 | custom fusion | bytes 50333696 | tf_op jit(solution)/shard_map/scatter | solution.py:80
  512.0 9.8 slice_bitcast_fusion
  521.8 514.1 %while.30 = (s32[]{:T(128)}, f32[1,1024]{1,0:T(1,128)S(1)}, f32[1,1024]{1,0:T(1,128)S(1)}, f32[1,1024,128]{2,1,0:T(8,128)S(1)}, s32[18]{0:T(128)S(1)}, /*index=5...) while((s32[]{:T(128)}, f32[1,1024]{1,0:T(1,128)S(1)}, ...), condition=%wide.region_10.11_spmd.clone, body=%wide.region_7.10_spmd.clone.sunk | while | flops 557346816 | bytes 14634959 | solution.py:151
  521.8 8.6 compare_select_fusion.26
  530.8 5.5 select_select_fusion.5
  537.7 5.5 select_select_fusion.4
  550.3 8.6 compare_select_fusion.26
  559.3 5.5 select_select_fusion.5
  566.3 5.5 select_select_fusion.4
  578.9 8.6 compare_select_fusion.26
  587.9 5.5 select_select_fusion.5
  594.8 5.5 select_select_fusion.4
  607.5 8.6 compare_select_fusion.26
  616.5 5.5 select_select_fusion.5
  623.4 5.5 select_select_fusion.4
  636.0 8.6 compare_select_fusion.26
  645.0 5.5 select_select_fusion.5
  652.0 5.5 select_select_fusion.4
  664.6 8.6 compare_select_fusion.26
  673.6 5.5 select_select_fusion.5
  680.5 5.5 select_select_fusion.4
  693.2 8.6 compare_select_fusion.26
  702.1 5.5 select_select_fusion.5
  709.1 5.5 select_select_fusion.4
  721.7 8.6 compare_select_fusion.26
  730.7 5.5 select_select_fusion.5
  737.7 5.5 select_select_fusion.4
  750.3 8.6 compare_select_fusion.26
  759.3 5.5 select_select_fusion.5
  766.2 5.5 select_select_fusion.4
  778.9 8.6 compare_select_fusion.26
  787.8 5.5 select_select_fusion.5
  794.8 5.5 select_select_fusion.4
  807.4 8.6 compare_select_fusion.26
  816.4 5.5 select_select_fusion.5
  823.3 5.5 select_select_fusion.4
  836.0 8.6 compare_select_fusion.26
  845.0 5.5 select_select_fusion.5
  851.9 5.5 select_select_fusion.4
  864.6 8.6 compare_select_fusion.26
  880.5 5.5 select_select_fusion.4
  893.1 8.6 compare_select_fusion.26
  909.0 5.5 select_select_fusion.4
  921.7 8.6 compare_select_fusion.26
  937.6 5.5 select_select_fusion.4
  950.2 8.6 compare_select_fusion.26
  966.2 5.5 select_select_fusion.4
  978.8 8.6 compare_select_fusion.26
  994.7 5.5 select_select_fusion.4
  1007.4 8.6 compare_select_fusion.26
  1023.3 5.5 select_select_fusion.4
  1036.8 9.5 all-gather.3
  1046.4 10.0 all-gather.4
  1056.4 9.9 all-gather.10.cloned.1.call-done
  1070.6 23.1 %all-gather.8.cloned.1.call-done = bf16[4,64,2048]{2,1,0:T(8,128)(2,1)} async-done(((bf16[4,16,2048]{2,1,0:T(8,128)(2,1)}), bf16[4,64,2048]{2,1,0:T(8,128)(2,1)}) %all-gather.8.cloned.1.call-update) | async-done | bytes 1048592 | tf_op jit(solution)/shard_map/all_gather | solution.py:163
  1098.5 30.5 %reduce-scatter.2.cloned.1.call-done = f32[4,64,128]{2,1,0:T(8,128)} async-done(((f32[4,64,1024]{2,1,0:T(8,128)}), f32[4,64,128]{2,1,0:T(8,128)}) %reduce-scatter.2.cloned.1.call-update) | async-done | bytes 131088 | tf_op jit(solution)/shard_map/reduce_scatter | solution.py:167
  (455 shorter events, 212.6 us)
Async XLA Ops:
  226.1 7.7 copy-start.1
  226.1 8.3 copy-start
  226.1 12.9 %copy-start.5 = (s32[64]{0:T(128)S(1)}, s32[64]{0:T(128)}, u32[]{:S(2)}) copy-start(s32[64]{0:T(128)} %param.18) | copy-start | bytes 772
  226.1 12.9 %copy-start.6 = (s32[64]{0:T(128)S(1)}, s32[64]{0:T(128)}, u32[]{:S(2)}) copy-start(s32[64]{0:T(128)} %param.19) | copy-start | bytes 772
  226.1 13.0 %copy-start.7 = (s32[16]{0:T(128)S(1)}, s32[16]{0:T(128)}, u32[]{:S(2)}) copy-start(s32[16]{0:T(128)} %param.15) | copy-start | bytes 196
  226.2 20.4 %copy-start.3 = (bf16[4,16,2,1,128]{4,2,3,1,0:T(2,128)(2,1)S(1)}, bf16[4,16,2,1,128]{4,2,3,1,0:T(2,128)(2,1)}, u32[]{:S(2)}) copy-start(bf16[4,16,2,1,128]{4,2,3,1,0:T(2,128)(2,1)} %param.21) | copy-start | bytes 98308
  226.2 191.0 %all-to-all-start.1 = ((bf16[4,16,2,8,64,128]{5,4,2,1,0,3:T(8,128)(2,1)}), bf16[4,16,2,8,64,128]{5,4,2,1,0,3:T(8,128)(2,1)}, u32[]{:S(2)}, u32[]{:S(2)}) async-start(bf16[4,16,2,8,64,128]{5,4,2,1,0,3:T(8,128)(2,1)} %copy.41), calls=%async_computation.1 | async-start | bytes 33554432 | tf_op jit(solution)/shard_map/all_to_all | solution.py:65
  233.8 832.5 %all-gather.10.cloned.1.call-start = ((), (), s32[]{:S(2)}) async-start(), calls=%async_computation.5 | async-start | bytes 2621440 | tf_op jit(solution)/shard_map/all_gather | solution.py:10
  1035.9 0.8 copy-start.2
  1036.8 56.9 %all-gather.8.cloned.1.call-start = ((), (), s32[]{:S(2)}) async-start(), calls=%async_computation.3 | async-start | bytes 1310720 | tf_op jit(solution)/shard_map/all_gather | solution.py:163
  1066.3 1.6 slice-start
  1070.5 58.5 %copy-start.4 = (bf16[4,64,128]{2,1,0:T(8,128)(2,1)S(1)}, bf16[4,64,128]{2,1,0:T(8,128)(2,1)}, u32[]{:S(2)}) copy-start(bf16[4,64,128]{2,1,0:T(8,128)(2,1)} %param.23) | copy-start | bytes 196612
  1070.5 58.5 %reduce-scatter.2.cloned.1.call-start = ((), (), s32[]{:S(2)}) async-start(), calls=%async_computation.4 | async-start | bytes 1179648 | tf_op jit(solution)/shard_map/reduce_scatter | solution.py:167
Sparse Core Ops, SparseCore 0:
  1036.9 29.3 all-gather.9
  1070.6 22.9 all-gather.7
  1098.6 30.3 reduce-scatter.1
where the time goes:
time: 1150 us; the launch traced here: 1140 us
  other arithmetic  404 us (35%)
  waiting for transfers between devices  234 us (20%)
  blocking collectives  207 us (18%)
  local copies, waits for them, and re-layouts  161 us (14%)
  matrix products  96.3 us (8%)
  between operations  14 us (1%)
  loops' own time  13.1 us (1%)
    gather x36, other arithmetic, shards(): query_pos = row_pos[query_row]  254 us
    all_to_all x1, blocking collectives, shards(): lax.all_to_all(outgoing, 'instance', split_axis=0, concat_axis=0, tiled=T...  187 us
    all_to_all x1, waiting for transfers between devices, shards(): lax.all_to_all(lax.all_to_all(outgoing, 'instance', split_axis=0, concat_...  170 us
    gather x180, other arithmetic, shards(): query_req = row_req[query_row]  106 us
    scatter x1, local copies, waits for them, and re-layouts, shards(): decode_pool.at[target]  74.4 us
    dot_general x18, matrix products, visit(): jnp.einsum('kqbu,bkud->kqd', probs.astype(jnp.bfloat16), val_blk, preferr...  53.3 us
    dot_general x18, matrix products, visit(): jnp.einsum('kqd,bkud->kqbu', query_h, key_blk, preferred_element_type=jnp...  37.7 us
    reduce_sum x18, other arithmetic, visit(): total = total * shrink + jnp.sum(probs, axis=(2, 3))  32.7 us
  transfers between devices with their start and end apart: 4, of which 4 were waited for; matrix products, arithmetic and copies ran while one was open for 1% of the time, Pallas kernels for 0%

commit v1 on v0

v1 whole, which is shorter than its diff:
```python
import functools

import jax
import jax.numpy as jnp
from jax import lax
from jax.experimental import pallas as pl
from jax.experimental.pallas import tpu as pltpu
from jax.sharding import PartitionSpec as P

MESH = pl.DeviceIdType.MESH
OTHERLEN = 12288
LOW = -1e30
MASKED = -2e30
NI, NL, NT = 4, 4, 8
NEAR = 6
FAR = 10
PAGES = NI * NEAR * NT
EXTRA = FAR * NT


def extra_kernel(p, g, src, dst, send_sem, recv_sem, fill_sem):
    i, l, t = (lax.axis_index(a) for a in ("instance", "layout", "tensor"))
    first = 1 if p == g else 0
    barrier = pltpu.get_barrier_semaphore()

    def peer(group, dt):
        return (group, l, lax.rem(t + dt, NT))

    def copy(k, dt):
        to = peer(g, dt)
        return pltpu.make_async_remote_copy(
            src_ref=src.at[k, :, to[2]],
            dst_ref=dst.at[k, dt],
            send_sem=send_sem.at[dt, k],
            recv_sem=recv_sem.at[dt, k],
            device_id=to,
            device_id_type=MESH,
        )

    @pl.when(i == g)
    def _():
        for dt in range(first, NT):
            pl.semaphore_signal(barrier, inc=1, device_id=peer(p, dt), device_id_type=MESH)

    @pl.when(i == p)
    def _():
        pl.semaphore_wait(barrier, NT - first)

        def send(k, c):
            for dt in range(first, NT):
                copy(k, dt).start()
            return c

        lax.fori_loop(0, FAR, send, 0)

    if p == g:

        @pl.when(i == g)
        def _():
            own = pltpu.make_async_copy(src.at[:, :, t], dst.at[:, 0], fill_sem.at[0])
            own.start()
            own.wait()

    @pl.when(i != g)
    def _():
        fills = [pltpu.make_async_copy(src.at[:, :, h], dst.at[:, h], fill_sem.at[h]) for h in range(NT)]
        for f in fills:
            f.start()
        for f in fills:
            f.wait()

    @pl.when(i == p)
    def _():
        def drain(k, c):
            for dt in range(first, NT):
                copy(k, dt).wait_send()
            return c

        lax.fori_loop(0, FAR, drain, 0)

    @pl.when(i == g)
    def _():
        def arrive(k, c):
            for dt in range(first, NT):
                copy(k, dt).wait_recv()
            return c

        lax.fori_loop(0, FAR, arrive, 0)


def move_extra(p, g, src):
    return pl.pallas_call(
        functools.partial(extra_kernel, p, g),
        out_shape=jax.ShapeDtypeStruct((FAR, NT, 2, 64, 128), jnp.bfloat16),
        in_specs=[pl.BlockSpec(memory_space=pl.ANY)],
        out_specs=pl.BlockSpec(memory_space=pl.ANY),
        scratch_shapes=[
            pltpu.SemaphoreType.DMA((NT, FAR)),
            pltpu.SemaphoreType.DMA((NT, FAR)),
            pltpu.SemaphoreType.DMA((NT,)),
        ],
        compiler_params=pltpu.CompilerParams(collective_id=1 + p * NI + g, has_side_effects=True),
    )(src)


def main_kernel(
    send,
    extra,
    weight,
    query,
    fresh,
    pick,
    order,
    pos,
    pos_x,
    pick_x,
    far,
    residual,
    pages,
    attn,
    recv,
    ext,
    w,
    q,
    qx,
    fkv,
    acc,
    ml,
    got,
    ctx,
    proj,
    red,
    zero,
    send_sem,
    recv_sem,
    own_sem,
    page_sem,
    w_sem,
    ext_sem,
    s1_sem,
    r1_sem,
    s2_sem,
    r2_sem,
    s4_sem,
    r4_sem,
):
    i, l, t = (lax.axis_index(a) for a in ("instance", "layout", "tensor"))
    scale = 128.0**-0.5

    def plane(di, dt):
        return (lax.rem(i + di, NI), l, lax.rem(t + dt, NT))

    def column(di, dl):
        return (lax.rem(i + di, NI), lax.rem(l + dl, NL), t)

    barrier = pltpu.get_barrier_semaphore()
    for di in range(NI):
        for dt in range(NT):
            if di or dt:
                pl.semaphore_signal(barrier, inc=1, device_id=plane(di, dt), device_id_type=MESH)
    for di in range(NI):
        for dl in range(1, NL):
            pl.semaphore_signal(barrier, inc=1, device_id=column(di, dl), device_id_type=MESH)

    w_copy = pltpu.make_async_copy(weight, w, w_sem)
    ext_copy = pltpu.make_async_copy(extra, ext, ext_sem)
    ext_copy.start()
    own = [pltpu.make_async_copy(send.at[0, k, :, t], recv.at[0, k, 0], own_sem.at[k]) for k in range(NEAR)]
    for c in own:
        c.start()
    pl.semaphore_wait(barrier, NI * NT - 1 + NI * (NL - 1))

    def page_copy(k, di, dt):
        to = plane(di, dt)
        return pltpu.make_async_remote_copy(
            src_ref=send.at[di, k, :, to[2]],
            dst_ref=recv.at[di, k, dt],
            send_sem=send_sem.at[di, k, dt],
            recv_sem=recv_sem.at[di, k, dt],
            device_id=to,
            device_id_type=MESH,
        )

    def pair(n):
        di = n % 4
        dz = (di + n // 8) % 4
        return di, dz * 2 + (n // 4) % 2

    def send_page(k, c):
        def one(n, c):
            di, dt = pair(n)

            @pl.when(n != 0)
            def _():
                page_copy(k, di, dt).start()

            return c

        return lax.fori_loop(0, NI * NT, one, c)

    lax.fori_loop(0, NEAR, send_page, 0)
    w_copy.start()

    sorted_q = jnp.dot(pick[...], query[...], preferred_element_type=jnp.float32).astype(jnp.bfloat16)
    sorted_x = jnp.dot(pick_x[...], query[...], preferred_element_type=jnp.float32).astype(jnp.bfloat16)
    fkv[...] = jnp.dot(pick[...], fresh[...], preferred_element_type=jnp.float32).astype(jnp.bfloat16)
    for h in range(16):
        for d in range(NI):
            q[d, h * 16 : (h + 1) * 16, :] = sorted_q[d * 16 : (d + 1) * 16, h * 128 : (h + 1) * 128]
        qx[h * 16 : (h + 1) * 16, :] = sorted_x[:, h * 128 : (h + 1) * 128]
    zero[...] = jnp.zeros_like(zero)

    def update(m, total, weighted, s, v):
        top = jnp.maximum(m, jnp.max(s, axis=1, keepdims=True))
        shrink = jnp.exp(m - top)
        p = jnp.exp(s - top)
        total = total * shrink + jnp.sum(p, axis=1, keepdims=True)
        weighted = weighted * shrink + jnp.dot(p.astype(jnp.bfloat16), v, preferred_element_type=jnp.float32)
        return top, total, weighted

    def dots(a, b):
        return lax.dot_general(a, b, (((1,), (1,)), ((), ())), preferred_element_type=jnp.float32) * scale

    ext_copy.wait()
    ext_out = pltpu.make_async_copy(ext, pages.at[pl.ds(NI * NEAR, FAR)], ext_sem)
    ext_out.start()

    def extra_step(k, carry):
        n = lax.broadcasted_iota(jnp.int32, (1, NT * 64), 1)
        ts = (t + NT - n // 64) % NT
        token = (((NEAR + k) * NT + ts) * NL + l) * 64 + n % 64
        s = dots(qx[...], ext[k, :, 0].reshape(NT * 64, 128))
        s = jnp.where(token < pos_x[...], s, MASKED)
        return update(*carry, s, ext[k, :, 1].reshape(NT * 64, 128))

    empty = (
        jnp.full((256, 1), LOW, jnp.float32),
        jnp.zeros((256, 1), jnp.float32),
        jnp.zeros((256, 128), jnp.float32),
    )
    mx, tx, ax = lax.fori_loop(0, FAR, extra_step, empty)

    a = lax.broadcasted_iota(jnp.int32, (256, 16), 0)
    b = lax.broadcasted_iota(jnp.int32, (256, 16), 1)
    visible = (a % 4 == b % 4) & (b // 4 <= (a // 4) % 4) & (l == 0)
    for d in range(NI):
        rows = slice(d * 16, (d + 1) * 16)
        s = jnp.where(visible, dots(q[d], fkv[rows, :128]), MASKED)
        start = (jnp.maximum(mx + far[d : d + 1, :1], LOW), tx, ax)
        start = (start[0], jnp.where(start[0] > LOW, tx, 0.0), jnp.where(start[0] > LOW, ax, 0.0))
        m, total, weighted = update(*start, s, fkv[rows, 128:])
        acc[d] = weighted
        ml[d, :, :64] = jnp.broadcast_to(m, (256, 64))
        ml[d, :, 64:] = jnp.broadcast_to(total, (256, 64))

    for c in own:
        c.wait()

    def visit(k, c):
        def request(d, c):
            for dt in range(NT):
                if dt:
                    page_copy(k, d, dt).wait_recv()
                else:

                    @pl.when(d != 0)
                    def _():
                        page_copy(k, d, dt).wait_recv()

            pltpu.make_async_copy(recv.at[d, k], pages.at[d * NEAR + k], page_sem.at[d, k]).start()
            n = lax.broadcasted_iota(jnp.int32, (1, NT * 64), 1)
            ts = (t + NT - n // 64) % NT
            token = ((k * NT + ts) * NL + l) * 64 + n % 64
            s = dots(q[d], recv[d, k, :, 0].reshape(NT * 64, 128))
            s = jnp.where(token < pos[d], s, MASKED)
            m, total, weighted = update(
                ml[d, :, :1], ml[d, :, 64:65], acc[d], s, recv[d, k, :, 1].reshape(NT * 64, 128)
            )
            acc[d] = weighted
            ml[d, :, :64] = jnp.broadcast_to(m, (256, 64))
            ml[d, :, 64:] = jnp.broadcast_to(total, (256, 64))
            return c

        return lax.fori_loop(0, NI, request, c)

    lax.fori_loop(0, NEAR, visit, 0)

    joins = []
    for dl in range(1, NL):
        to = column(0, dl)
        for part, ref in enumerate((acc, ml)):
            joins.append(
                pltpu.make_async_remote_copy(
                    src_ref=ref.at[to[1]],
                    dst_ref=got.at[dl - 1, part],
                    send_sem=s1_sem.at[dl - 1, part],
                    recv_sem=r1_sem.at[dl - 1, part],
                    device_id=to,
                    device_id_type=MESH,
                )
            )
    for c in joins:
        c.start()
    for c in joins:
        c.wait_recv()
    parts = [(acc[l], ml[l])] + [(got[n, 0], got[n, 1]) for n in range(NL - 1)]
    top = functools.reduce(jnp.maximum, [p[1][:, :1] for p in parts])
    total = sum(p[1][:, 64:65] * jnp.exp(p[1][:, :1] - top) for p in parts)
    weighted = sum(p[0] * jnp.exp(p[1][:, :1] - top) for p in parts)
    joined = (weighted / total).astype(jnp.bfloat16)
    mine = i * NL + l
    for h in range(16):
        ctx[mine, :, h * 128 : (h + 1) * 128] = joined[h * 16 : (h + 1) * 16, :]

    spread = []
    for di in range(NI):
        for dl in range(NL):
            if di or dl:
                spread.append(
                    pltpu.make_async_remote_copy(
                        src_ref=ctx.at[mine],
                        dst_ref=ctx.at[mine],
                        send_sem=s2_sem.at[di, dl],
                        recv_sem=r2_sem.at[di, dl],
                        device_id=column(di, dl),
                        device_id_type=MESH,
                    )
                )
    for c in spread:
        c.start()
    w_copy.wait()
    for c in spread:
        c.wait_recv()
    context = jnp.dot(order[...], ctx[...].reshape(256, 2048), preferred_element_type=jnp.float32)
    context = context.astype(jnp.bfloat16)
    for n in range(NT):
        proj[n] = jnp.dot(context, w[:, n * 128 : (n + 1) * 128], preferred_element_type=jnp.float32)
    sums = []
    for dt in range(1, NT):
        to = plane(0, dt)
        sums.append(
            pltpu.make_async_remote_copy(
                src_ref=proj.at[to[2]],
                dst_ref=red.at[dt - 1],
                send_sem=s4_sem.at[dt - 1],
                recv_sem=r4_sem.at[dt - 1],
                device_id=to,
                device_id_type=MESH,
            )
        )
    for c in sums:
        c.start()

    total = proj[t] + residual[...].astype(jnp.float32)
    for n, c in enumerate(sums):
        c.wait_recv()
        total = total + red[n]
    attn[...] = total

    zero_out = pltpu.make_async_copy(zero, pages.at[NI * NEAR + FAR], own_sem.at[0])
    zero_out.start()
    zero_out.wait()
    ext_out.wait()
    for c in joins + spread + sums:
        c.wait_send()

    def drain(k, c):
        def one(n, c):
            di, dt = pair(n)

            @pl.when(n != 0)
            def _():
                page_copy(k, di, dt).wait_send()

            return c

        for d in range(NI):
            pltpu.make_async_copy(recv.at[d, k], pages.at[d * NEAR + k], page_sem.at[d, k]).wait()
        return lax.fori_loop(0, NI * NT, one, c)

    lax.fori_loop(0, NEAR, drain, 0)


def run_main(*args):
    hbm, vmem = pl.BlockSpec(memory_space=pl.ANY), pl.BlockSpec(memory_space=pltpu.VMEM)
    bf, f32, dma = jnp.bfloat16, jnp.float32, pltpu.SemaphoreType.DMA
    return pl.pallas_call(
        main_kernel,
        out_shape=(
            jax.ShapeDtypeStruct((NI * NEAR + FAR + 1, NT, 2, 64, 128), bf),
            jax.ShapeDtypeStruct((256, 128), f32),
        ),
        in_specs=[hbm] * 3 + [vmem] * 9,
        out_specs=(hbm, vmem),
        scratch_shapes=[
            pltpu.VMEM((NI, NEAR, NT, 2, 64, 128), bf),
            pltpu.VMEM((FAR, NT, 2, 64, 128), bf),
            pltpu.VMEM((2048, 1024), bf),
            pltpu.VMEM((NI, 256, 128), bf),
            pltpu.VMEM((256, 128), bf),
            pltpu.VMEM((64, 256), bf),
            pltpu.VMEM((NI, 256, 128), f32),
            pltpu.VMEM((NI, 256, 128), f32),
            pltpu.VMEM((NL - 1, 2, 256, 128), f32),
            pltpu.VMEM((NI * NL, 16, 2048), bf),
            pltpu.VMEM((NT, 256, 128), f32),
            pltpu.VMEM((NT - 1, 256, 128), f32),
            pltpu.VMEM((NT, 2, 64, 128), bf),
            dma((NI, NEAR, NT)),
            dma((NI, NEAR, NT)),
            dma((NEAR,)),
            dma((NI, NEAR)),
            dma,
            dma,
            dma((NL - 1, 2)),
            dma((NL - 1, 2)),
            dma((NI, NL)),
            dma((NI, NL)),
            dma((NT - 1,)),
            dma((NT - 1,)),
        ],
        compiler_params=pltpu.CompilerParams(
            collective_id=0, has_side_effects=True, vmem_limit_bytes=48 * 1024 * 1024
        ),
    )(*args)


def shards(
    prefill_pool,
    lengths,
    src_table,
    dst_table,
    row_request,
    positions,
    queries,
    step_key_value,
    out_weight,
    residual,
):
    inst, lay, ten = (lax.axis_index(a) for a in ("instance", "layout", "tensor"))
    src_dev = prefill_pool.shape[0]
    slots = 288
    npages = (lengths + 63) // 64
    src_grp = src_table[:, 0] // (src_dev * NL * NT)
    dec_grp = dst_table[:, 0] // (slots * NL)
    place = jnp.arange(4, dtype=jnp.int32)
    k16 = jnp.arange(16, dtype=jnp.int32)

    rank = (inst * NL + lay) * NT + ten
    own_src = lax.dynamic_slice(src_table.reshape(16, 16, NT, NL), (0, 0, ten, lay), (16, 16, 1, 1)).reshape(16, 16)
    own_src = jnp.clip(own_src - rank * src_dev, 0, src_dev - 1)
    to_place = (src_grp[None, :] == inst) & ((dec_grp[None, :] - inst) % NI == place[:, None])
    slot = jnp.sum(jnp.where(to_place[:, :, None], own_src[None], 0), axis=1)
    longest = lengths == jnp.max(lengths)
    long_slot = jnp.sum(jnp.where(longest[:, None], own_src, 0), axis=0)
    long_src = jnp.sum(jnp.where(longest, src_grp, 0))
    long_dec = jnp.sum(jnp.where(longest, dec_grp, 0))
    send_extra = prefill_pool[long_slot[NEAR:]]
    send = prefill_pool[slot[:, :NEAR]]
    extra = lax.switch(
        long_src * NI + long_dec,
        [functools.partial(move_extra, p, g) for p in range(NI) for g in range(NI)],
        send_extra,
    )

    row_src = jnp.sum(jnp.where(row_request[:, None] == k16[None, :], src_grp[None, :], 0), axis=1)
    rows = jnp.arange(64, dtype=jnp.int32)
    row_grp = rows // 16
    row_place = (row_grp - row_src) % NI
    earlier = (row_request[:, None] == row_request[None, :]) & (rows[None, :] < rows[:, None])
    row_rank = jnp.sum(earlier.astype(jnp.int32), axis=1)
    step = jnp.arange(4, dtype=jnp.int32)
    flat = (row_grp * 64 + row_place * 16 + row_rank)[None, :] + step[:, None] * 4
    order = (flat.reshape(256, 1) == jnp.arange(256, dtype=jnp.int32)[None, :]).astype(jnp.bfloat16)
    local = lax.dynamic_slice_in_dim(row_place * 16 + row_rank, inst * 16, 16)
    local = local[None, :] + step[:, None] * 4
    pick = (jnp.arange(64, dtype=jnp.int32)[:, None] == local.reshape(1, 64)).astype(jnp.bfloat16)
    local_pos = lax.dynamic_slice_in_dim(positions, inst * 16, 16)
    local_place = lax.dynamic_slice_in_dim(row_place, inst * 16, 16)
    local_rank = lax.dynamic_slice_in_dim(row_rank, inst * 16, 16)
    hit = (local_place[None, None, :] == place[:, None, None]) & (local_rank[None, None, :] == place[None, :, None])
    pos = jnp.sum(jnp.where(hit, local_pos[None, None, :], 0), axis=2)
    pos = jnp.broadcast_to(pos[:, None, :], (4, 64, 4)).reshape(4, 256, 1)
    here = (long_dec == inst) & ((inst - long_src) % NI == place)
    pos_x = jnp.sum(jnp.where(here[:, None, None], pos, 0), axis=0)
    pick_x = jnp.sum(jnp.where(here[:, None, None], pick.reshape(4, 16, 64), 0), axis=0).astype(jnp.bfloat16)
    far = jnp.broadcast_to(jnp.where(here, 0.0, 2 * LOW)[:, None], (4, 128)).astype(jnp.float32)

    pages, attn = run_main(
        send,
        extra,
        out_weight,
        queries.reshape(64, 2048),
        step_key_value.reshape(64, 256),
        pick,
        order,
        pos,
        pos_x,
        pick_x,
        far,
        residual.reshape(256, 128),
    )

    own_dst = lax.dynamic_slice_in_dim(dst_table.reshape(16, 16, NT, NL), lay, 1, 3).reshape(16, 16, NT)
    from_place = (dec_grp[None, :] == inst) & ((inst - src_grp[None, :]) % NI == place[:, None])
    target = jnp.sum(jnp.where(from_place[:, :, None, None], own_dst[None], 0), axis=1)
    target = target - (inst * NL + lay) * slots
    count = jnp.sum(jnp.where(from_place, npages[None, :], 0), axis=1)
    t8 = jnp.arange(NT, dtype=jnp.int32)
    page = (k16[:, None] * NT + t8[None, :]) * NL + lay
    live = page[None] < count[:, None, None]
    dt = (ten - t8) % NT
    near = (place[:, None, None] * NEAR + k16[None, :, None]) * NT + dt[None, None, :]
    beyond = (NI * NEAR + k16[None, :, None] - NEAR) * NT + dt[None, None, :]
    source = jnp.where(k16[None, :, None] < NEAR, near, beyond)
    source = jnp.where(live, source, -1).reshape(1, 512)
    match = target.reshape(1, 512) == jnp.arange(slots, dtype=jnp.int32)[:, None]
    index = jnp.max(jnp.where(match, source, -1), axis=1)
    index = jnp.where(index < 0, (NI * NEAR + FAR) * NT, index)
    pool = pages.reshape((NI * NEAR + FAR + 1) * NT, 2, 64, 128)[index]
    return pool.reshape(slots, 2, 1, 64, 128), attn.reshape(4, 64, 128)


def solution(mesh):
    in_specs = (
        P(("instance", "layout", "tensor"), None, None, None, None),
        P(),
        P(),
        P(),
        P(),
        P(),
        P(None, "instance", "tensor"),
        P(None, "instance", None, "tensor", None),
        P("tensor", ("instance", "layout")),
        P(None, None, ("instance", "layout", "tensor")),
    )
    out_specs = (
        P(("instance", "layout"), None, "tensor", None, None),
        P(None, None, ("instance", "layout", "tensor")),
    )
    return jax.shard_map(shards, mesh=mesh, in_specs=in_specs, out_specs=out_specs, check_vma=False)
```

time: 1150 us -> 243 us (0.21); the launches traced: 1140 us -> 243 us
  other arithmetic: 404 us -> 9.91 us
  waiting for transfers between devices: 234 us -> 0 us
  blocking collectives: 207 us -> 0 us
  Pallas kernels: 0 us -> 196 us
  local copies, waits for them, and re-layouts: 161 us -> 32.9 us
  matrix products: 96.3 us -> 0 us
  loops' own time: 13.1 us -> 0.24 us
    gather x218 -> x3, other arithmetic: 360 us -> 0.02 us  [the longest x1 0.01 us: shards(): send_extra = prefill_pool[long_slot[NEAR:]]]
    pallas_call x0 -> x2, Pallas kernels: none -> 196 us  [the longest x1 193 us: run_main(): pl.pallas_call(main_kernel, out_shape=(jax.ShapeDtypeStruct((NI * NEAR +...]
    all_to_all x1 -> x0, blocking collectives: 187 us -> none  [shards(): lax.all_to_all(outgoing, 'instance', split_axis=0, concat_axis=0, tiled=T...]
    all_to_all x1 -> x0, waiting for transfers between devices: 170 us -> none  [shards(): lax.all_to_all(lax.all_to_all(outgoing, 'instance', split_axis=0, concat_...]
    dot_general x39 -> x0, matrix products: 96.3 us -> none  [the longest x18 53.3 us: visit(): jnp.einsum('kqbu,bkud->kqd', probs.astype(jnp.bfloat16), val_blk, preferr...]
    scatter x3 -> x0, local copies, waits for them, and re-layouts: 79.5 us -> none  [the longest x1 74.4 us: shards(): decode_pool.at[target]]
    all_gather x2 -> x0, waiting for transfers between devices: 33 us -> none  [the longest x1 23.1 us: shards(): lax.all_gather(context, 'instance', axis=1, tiled=True)]
    reduce_scatter x1 -> x0, waiting for transfers between devices: 30.5 us -> none  [shards(): lax.psum_scatter(projected, 'tensor', scatter_dimension=2, tiled=True)]
  transfers between devices with their start and end apart: 4 -> 0, of which waited for: 4 -> 0; matrix products, arithmetic and copies ran while one was open for 1% -> 0% of each run, Pallas kernels for 0% -> 0%
where the time goes in v1:
time: 243 us
  Pallas kernels  196 us (81%)
  local copies, waits for them, and re-layouts  32.9 us (14%)
  other arithmetic  9.91 us (4%)
  between operations  3.61 us (1%)
    pallas_call x1, Pallas kernels, run_main(): pl.pallas_call(main_kernel, out_shape=(jax.ShapeDtypeStruct((NI * NEAR +...  193 us
    gather x1, local copies, waits for them, and re-layouts, shards(): pool = pages.reshape((NI * NEAR + FAR + 1) * NT, 2, 64, 128)[index]  14 us
    gather x1, local copies, waits for them, and re-layouts, shards(): send = prefill_pool[slot[:, :NEAR]]  8.22 us

profile of v1, /device:TPU:1, one launch (start us, length us, event | category | flops | bytes accessed | tf_op | source)
XLA Modules:
  0.0 242.7 jit_solution(13789330267698480248)
XLA Ops:
  0.6 0.8 divide_reduce_fusion.1
  1.5 0.8 fusion.8
  2.3 0.7 select_reduce_fusion.5
  3.0 0.9 convert_reduce_fusion
  4.0 0.1 dynamic_slice.20
  4.0 0.1 dynamic_slice.21
  4.1 0.7 dynamic_slice.22
  4.9 0.2 select_reduce_fusion.4
  5.0 0.2 reshape.596.pos
  5.2 0.8 divide_reduce_fusion
  6.0 0.8 fusion.7
  6.8 1.3 reduce_max.20
  8.1 2.0 select_reduce_fusion.8
  11.5 0.1 select_reduce_fusion.2
  11.6 0.1 reduce_sum.116.pos_x
  11.7 0.1 dynamic_slice.19
  11.8 0.1 broadcast_add_fusion.2
  11.9 0.1 add.279
  12.0 0.1 fusion.4.pick_x
  12.1 0.1 broadcast_in_dim.237.far
  12.1 0.9 copy.26
  13.0 0.1 copy.33
  13.1 0.1 select_reduce_fusion.6
  13.2 0.1 compare_select_fusion.3
  13.3 4.7 %gather_fusion.1 = bf16[10,2,8,64,128]{4,3,2,1,0:T(8,128)(2,1)S(1)} fusion(bf16[36,2,8,64,128]{4,3,2,1,0:T(8,128)(2,1)} %param.26, s32[1024]{0:T(1024)S(1)} %pad_clamp_fusion.1), kind=kCustom, calls=%fused_computation.1 | custom fusion | bytes 5242920 | tf_op jit(solution)/shard_map/gather | solution.py:458
  19.4 3.3 %conditional.1 = (bf16[10,8,2,64,128]{4,3,2,1,0:T(8,128)(2,1)}) conditional(s32[]{:T(128)} %clamp.9, bf16[10,2,8,64,128]{4,3,2,1,0:T(8,128)(2,1)S(1)} %gather_fusion.1, bf16[10,2,8,64,128]{4,3,2,1,0:T(8,128)(2,1)S(1)} %gather_fusion.1, bf16[10,2,8,64,128]{4,3,2,1,0:T(8,128)(2,1)S(1)} %gather_fusion.1, ...), branch_computations={%region_5.6_spmd, %region_6.7_spmd, %region_7.8_spmd, %region_8.9_... | conditional | bytes 8 | solution.py:460
  19.4 3.1 %branch_9_fun.1 = bf16[10,8,2,64,128]{4,3,2,1,0:T(8,128)(2,1)} custom-call(bf16[10,2,8,64,128]{4,3,2,1,0:T(8,128)(2,1)S(1)} %src.9), custom_call_target="tpu_custom_call" | custom-call | tf_op jit(solution)/shard_map/cond/branch_9_fun/pallas_call | solution.py:92
  22.7 0.1 select_reduce_fusion.3
  22.8 0.1 reshape.571
  22.9 0.0 copy-start.4
  22.9 0.0 copy-start.1
  23.0 0.0 copy-start.2
  23.0 8.2 %gather_fusion = bf16[24,2,8,64,128]{4,3,2,1,0:T(8,128)(2,1)} fusion(bf16[36,2,8,64,128]{4,3,2,1,0:T(8,128)(2,1)} %param.26, s32[1024]{0:T(1024)S(1)} %pad_clamp_fusion.2), kind=kCustom, calls=%fused_computation | custom fusion | bytes 12583008 | tf_op jit(solution)/shard_map/gather | solution.py:459
  31.2 0.1 broadcast_add_fusion.1
  31.3 0.1 add.285
  31.4 0.1 fusion.order
  31.5 0.0 copy-done.4
  31.5 0.0 copy-done.1
  31.5 0.0 copy-done.2
  31.5 0.0 copy-start
  31.5 2.2 copy-done
  33.7 0.0 copy-start.3
  33.7 193.0 %shard_map.113 = (bf16[35,8,2,64,128]{4,3,2,1,0:T(8,128)(2,1)}, f32[256,128]{1,0:T(8,128)S(1)}) custom-call(bf16[4,6,2,8,64,128]{5,4,3,2,1,0:T(8,128)(2,1)} %bitcast.22, bf16[10,8,2,64,128]{4,3,2,1,0:T(8,128)(2,1)} %get-tuple-element.64.extra, bf16[2048,1024]{1,0:T(8,128)(2,1)S(1)} %copy-done, bf16[64,2048]{1,0:T(8,128)(2,1)S(1)} %bitcast.18, ...), custom_call_target="tpu_custom_call" | custom-call | tf_op jit(solution)/shard_map/pallas_call | solution.py:387
  226.7 0.1 select_reduce_fusion.7
  226.8 0.1 multiply_add_fusion
  226.9 0.1 add_multiply_fusion
  227.0 0.1 select_select_fusion
  227.1 0.1 select_n.225
  227.2 0.0 copy-done.3
  227.2 0.1 copy.30
  227.3 0.1 constant_dynamic-slice_fusion
  227.4 0.1 copy.31
  227.5 0.1 select_reduce_fusion.1
  227.7 0.1 copy.32
  227.7 0.1 sub.94
  227.8 0.2 select_reduce_fusion
  228.1 14.0 %gather_fusion.2 = bf16[288,2,64,128]{3,2,1,0:T(8,128)(2,1)} fusion(bf16[280,2,64,128]{3,2,1,0:T(8,128)(2,1)} %bitcast.23, s32[1024]{0:T(1024)S(1)} %pad_clamp_fusion), kind=kCustom, calls=%fused_computation.2 | custom fusion | bytes 18875520 | tf_op jit(solution)/shard_map/gather | solution.py:520
  242.1 0.7 copy.54
  (24 shorter events, 0.2 us)
Async XLA Ops:
  22.9 8.5 %copy-start.4 = (bf16[4,16,2,1,128]{4,2,3,1,0:T(2,128)(2,1)S(1)}, bf16[4,16,2,1,128]{4,2,3,1,0:T(2,128)(2,1)}, u32[]{:S(2)}) copy-start(bf16[4,16,2,1,128]{4,2,3,1,0:T(2,128)(2,1)} %param.33) | copy-start | bytes 98308
  22.9 8.6 %copy-start.1 = (bf16[4,16,2048]{2,1,0:T(8,128)(2,1)S(1)}, bf16[4,16,2048]{2,1,0:T(8,128)(2,1)}, u32[]{:S(2)}) copy-start(bf16[4,16,2048]{2,1,0:T(8,128)(2,1)} %param.32) | copy-start | bytes 786436
  23.0 8.5 %copy-start.2 = (bf16[4,64,128]{2,1,0:T(8,128)(2,1)S(1)}, bf16[4,64,128]{2,1,0:T(8,128)(2,1)}, u32[]{:S(2)}) copy-start(bf16[4,64,128]{2,1,0:T(8,128)(2,1)} %param.35) | copy-start | bytes 196612
  31.5 2.2 copy-start
  33.7 193.5 %copy-start.3 = (s32[16,512]{1,0:T(8,128)S(1)}, s32[16,512]{1,0:T(8,128)}, u32[]{:S(2)}) copy-start(s32[16,512]{1,0:T(8,128)} %param.29) | copy-start | bytes 98308

commit v2 on v1

v2 whole, which is shorter than its diff:
```python
import functools

import jax
import jax.numpy as jnp
from jax import lax
from jax.experimental import pallas as pl
from jax.experimental.pallas import tpu as pltpu
from jax.sharding import PartitionSpec as P

MESH = pl.DeviceIdType.MESH
LOW = -1e30
MASKED = -2e30
NI, NL, NT = 4, 4, 8
NEAR = 6
FAR = 10
LONGEST = 32768
SRC = 36
SLOTS = 288
GROUP = 1152


def routes(p, g):
    way = (g - p) % NI
    if way == 0:
        return [(0, FAR, [])]
    if way == 2:
        return [(0, FAR // 2, [(p + 1) % NI]), (FAR // 2, FAR, [(p - 1) % NI])]
    return [(0, 6, []), (6, FAR, [(p - way) % NI, (p - 2 * way) % NI])]


def find(lengths):
    return functools.reduce(lambda best, r: jnp.where(lengths[r] == LONGEST, r, best), range(16), jnp.int32(0))


def extra_kernel(p, g, lengths, table, pool, dst, held, packed, hop, zero, send_sem, recv_sem, hop_send, hop_recv, fill_sem):
    i, l, t = (lax.axis_index(a) for a in ("instance", "layout", "tensor"))
    barrier = pltpu.get_barrier_semaphore()

    def hop_copy(k, half, src, to):
        return pltpu.make_async_remote_copy(
            src_ref=src,
            dst_ref=hop.at[k, half],
            send_sem=hop_send.at[k, half],
            recv_sem=hop_recv.at[k, half],
            device_id=(to, l, t),
            device_id_type=MESH,
        )

    def last_copy(k, head, src):
        dt = lax.rem(head - t + NT, NT)
        return pltpu.make_async_remote_copy(
            src_ref=src,
            dst_ref=dst.at[k, dt],
            send_sem=send_sem.at[dt, k],
            recv_sem=recv_sem.at[dt, k],
            device_id=(g, l, head),
            device_id_type=MESH,
        )

    first = 1 if p == g else 0

    for lo, hi, via in routes(p, g):
        nodes = [p] + via

        @pl.when(i == g)
        def _():
            for dt in range(first, NT):
                to = (nodes[-1], l, lax.rem(t + dt, NT))
                pl.semaphore_signal(barrier, inc=1, device_id=to, device_id_type=MESH)

        for before, after in zip(nodes, via):

            @pl.when(i == after)
            def _():
                pl.semaphore_signal(barrier, inc=1, device_id=(before, l, t), device_id_type=MESH)

    @pl.when(i == p)
    def _():
        load = pltpu.make_async_copy(pool, held, fill_sem.at[0])
        load.start()
        pl.semaphore_wait(barrier, sum(1 if via else NT - first for _, _, via in routes(p, g)))
        load.wait()
        request = find(lengths)
        rank = (i * NL + l) * NT + t

        def pack(k):
            slot = table[request, ((NEAR + k) * NT + t) * NL + l] - rank * SRC
            packed[k] = held[jnp.clip(slot, 0, SRC - 1)]

        def direct(k, c):
            pack(k)
            for dt in range(first, NT):
                head = lax.rem(t + dt, NT)
                last_copy(k, head, packed.at[k, :, head]).start()
            return c

        def relayed(to, k, c):
            pack(k)
            for half in range(2):
                hop_copy(k, half, packed.at[k, :, half * 4 : half * 4 + 4], to).start()
            return c

        for lo, hi, via in reversed(routes(p, g)):
            lax.fori_loop(lo, hi, functools.partial(relayed, via[0]) if via else direct, 0)

    for lo, hi, via in routes(p, g):
        for n, node in enumerate(via):

            @pl.when(i == node)
            def _():
                pl.semaphore_wait(barrier, 1 if n + 1 < len(via) else NT)

                def forward(k, c):
                    for half in range(2):
                        hop_copy(k, half, hop.at[k, half], node).wait_recv()
                        if n + 1 < len(via):
                            hop_copy(k, half, hop.at[k, half], via[n + 1]).start()
                        else:
                            for hh in range(4):
                                h = lax.rem(t + hh, 4)
                                last_copy(k, half * 4 + h, hop.at[k, half, :, h]).start()
                    return c

                lax.fori_loop(lo, hi, forward, 0)

    if p == g:

        @pl.when(i == g)
        def _():
            own = pltpu.make_async_copy(packed.at[:, :, t], dst.at[:, 0], fill_sem.at[0])
            own.start()
            own.wait()

    @pl.when(i != g)
    def _():
        zero[...] = jnp.zeros_like(zero)
        fills = [pltpu.make_async_copy(zero, dst.at[k], fill_sem.at[k]) for k in range(FAR)]
        for f in fills:
            f.start()
        for f in fills:
            f.wait()

    for lo, hi, via in routes(p, g):
        nodes = [p] + via
        for n, node in enumerate(nodes):

            @pl.when(i == node)
            def _():
                def drain(k, c):
                    if n + 1 < len(nodes):
                        for half in range(2):
                            hop_copy(k, half, hop.at[k, half], node).wait_send()
                    else:
                        for dt in range(first, NT):
                            head = lax.rem(t + dt, NT)
                            last_copy(k, head, packed.at[k, :, head]).wait_send()
                    return c

                lax.fori_loop(lo, hi, drain, 0)

    @pl.when(i == g)
    def _():
        def arrive(k, c):
            for dt in range(first, NT):
                head = lax.rem(t + dt, NT)
                last_copy(k, head, packed.at[k, :, head]).wait_recv()
            return c

        lax.fori_loop(0, FAR, arrive, 0)


def move_extra(p, g, lengths, table, pool):
    smem, hbm = pl.BlockSpec(memory_space=pltpu.SMEM), pl.BlockSpec(memory_space=pl.ANY)
    bf, dma = jnp.bfloat16, pltpu.SemaphoreType.DMA
    return pl.pallas_call(
        functools.partial(extra_kernel, p, g),
        out_shape=jax.ShapeDtypeStruct((FAR, NT, 2, 64, 128), bf),
        in_specs=[smem, smem, hbm],
        out_specs=hbm,
        scratch_shapes=[
            pltpu.VMEM((SRC, 2, NT, 64, 128), bf),
            pltpu.VMEM((FAR, 2, NT, 64, 128), bf),
            pltpu.VMEM((FAR, 2, 2, 4, 64, 128), bf),
            pltpu.VMEM((NT, 2, 64, 128), bf),
            dma((NT, FAR)),
            dma((NT, FAR)),
            dma((FAR, 2)),
            dma((FAR, 2)),
            dma((FAR,)),
        ],
        compiler_params=pltpu.CompilerParams(
            collective_id=1 + p * NI + g, has_side_effects=True, vmem_limit_bytes=32 * 1024 * 1024
        ),
    )(lengths, table, pool)


def main_kernel(
    table,
    target,
    lengths,
    row_request,
    positions,
    pool,
    extra,
    weight,
    target_v,
    query,
    fresh,
    residual,
    pages,
    attn,
    index,
    held,
    send,
    recv,
    ext,
    w,
    q,
    qx,
    fkv,
    pos,
    acc,
    ml,
    got,
    ctx,
    proj,
    red,
    zero,
    send_sem,
    recv_sem,
    own_sem,
    page_sem,
    w_sem,
    ext_sem,
    pool_sem,
    s1_sem,
    r1_sem,
    s2_sem,
    r2_sem,
    s4_sem,
    r4_sem,
):
    i, l, t = (lax.axis_index(a) for a in ("instance", "layout", "tensor"))
    scale = 128.0**-0.5

    def plane(di, dt):
        return (lax.rem(i + di, NI), l, lax.rem(t + dt, NT))

    def column(di, dl):
        return (lax.rem(i + di, NI), lax.rem(l + dl, NL), t)

    barrier = pltpu.get_barrier_semaphore()
    load = pltpu.make_async_copy(pool, held, pool_sem)
    load.start()
    for di in range(NI):
        for dt in range(NT):
            if di or dt:
                pl.semaphore_signal(barrier, inc=1, device_id=plane(di, dt), device_id_type=MESH)
    for di in range(NI):
        for dl in range(1, NL):
            pl.semaphore_signal(barrier, inc=1, device_id=column(di, dl), device_id_type=MESH)

    w_copy = pltpu.make_async_copy(weight, w, w_sem)
    ext_copy = pltpu.make_async_copy(extra, ext, ext_sem)
    ext_copy.start()
    own = [pltpu.make_async_copy(send.at[0, k, :, t], recv.at[0, k, 0], own_sem.at[k]) for k in range(NEAR)]

    out_req = [jnp.int32(0)] * NI
    in_req = [jnp.int32(0)] * NI
    for r in range(16):
        src_r, dst_r = lax.div(table[r, 0], GROUP), lax.div(target[r, 0], GROUP)
        for d in range(NI):
            out_req[d] = jnp.where((src_r == i) & (dst_r == lax.rem(i + d, NI)), r, out_req[d])
            in_req[d] = jnp.where((dst_r == i) & (src_r == lax.rem(i + NI - d, NI)), r, in_req[d])
    rank = (i * NL + l) * NT + t
    pl.semaphore_wait(barrier, NI * NT - 1 + NI * (NL - 1))
    load.wait()

    def page_copy(k, di, dt):
        to = plane(di, dt)
        return pltpu.make_async_remote_copy(
            src_ref=send.at[di, k, :, to[2]],
            dst_ref=recv.at[di, k, dt],
            send_sem=send_sem.at[di, k, dt],
            recv_sem=recv_sem.at[di, k, dt],
            device_id=to,
            device_id_type=MESH,
        )

    def pair(n):
        di = n % 4
        dz = (di + n // 8) % 4
        return di, dz * 2 + (n // 4) % 2

    def send_page(k, c):
        for d in range(NI):
            slot = table[out_req[d], (k * NT + t) * NL + l] - rank * SRC
            send[d, k] = held[jnp.clip(slot, 0, SRC - 1)]

        def one(n, c):
            di, dt = pair(n)

            @pl.when(n != 0)
            def _():
                page_copy(k, di, dt).start()

            return c

        return lax.fori_loop(0, NI * NT, one, c)

    lax.fori_loop(0, NEAR, send_page, 0)
    w_copy.start()

    for c in own:
        c.start()

    def places(group):
        count, found = [jnp.int32(0)] * NI, []
        for n in range(16):
            request = row_request[group * 16 + n]
            d = lax.rem(group - lax.div(table[request, 0], GROUP) + NI, NI)
            rank = functools.reduce(lambda x, m: jnp.where(d == m, count[m], x), range(1, NI), count[0])
            count = [jnp.where(d == m, count[m] + 1, count[m]) for m in range(NI)]
            found.append((d, rank))
        return found

    def one_hot(found, by, plain):
        step = plain // 16
        hit = functools.reduce(
            jnp.logical_or, [(plain % 16 == n) & (by - step * 4 == d * 16 + rank) for n, (d, rank) in enumerate(found)]
        )
        return jnp.where(hit, 1.0, 0.0).astype(jnp.bfloat16)

    down = lax.broadcasted_iota(jnp.int32, (64, 64), 0)
    across = lax.broadcasted_iota(jnp.int32, (64, 64), 1)
    here = places(i)
    pick = one_hot(here, down, across)

    sorted_q = jnp.dot(pick, query[...], preferred_element_type=jnp.float32).astype(jnp.bfloat16)
    fkv[...] = jnp.dot(pick, fresh[...], preferred_element_type=jnp.float32).astype(jnp.bfloat16)
    for h in range(16):
        for d in range(NI):
            q[d, h * 16 : (h + 1) * 16, :] = sorted_q[d * 16 : (d + 1) * 16, h * 128 : (h + 1) * 128]
    in_row = lax.broadcasted_iota(jnp.int32, (256, 128), 0) % 4
    flag = [jnp.where(lengths[in_req[d]] == LONGEST, 1, 0) for d in range(NI)]
    qx[...] = jnp.zeros_like(qx)
    pos[NI] = jnp.zeros((256, 128), jnp.int32)
    for d in range(NI):
        seen = [jnp.int32(0)] * 4
        for n, (place, rank) in enumerate(here):
            seen = [jnp.where((place == d) & (rank == m), positions[i * 16 + n], seen[m]) for m in range(4)]
        pos[d] = functools.reduce(lambda x, m: jnp.where(in_row == m, seen[m], x), range(1, 4), jnp.full((256, 128), seen[0]))
        pos[NI] += pos[d] * flag[d]
        qx[...] = jnp.where(jnp.full((256, 128), flag[d]) == 1, q[d].astype(jnp.float32), qx[...])

    slot_of = lax.broadcasted_iota(jnp.int32, (384, 512), 0)
    j = lax.broadcasted_iota(jnp.int32, (1, 512), 1)
    k, dt = j // 32, (t - j // 4 + 2 * 512) % NT
    found = jnp.full((384, 512), -1, jnp.int32)
    for d in range(NI):
        page = jnp.where(k < NEAR, (d * NEAR + k) * NT + dt, (NI * NEAR + k - NEAR) * NT + dt)
        goes = (j % NL == l) & (j * 64 < lengths[in_req[d]])
        to = jnp.where(goes, target_v[pl.ds(in_req[d], 1), :] - (i * NL + l) * SLOTS, -1)
        found = jnp.where(slot_of == to, page, found)
    found = jnp.max(found, axis=1, keepdims=True)
    found = jnp.where(found < 0, (NI * NEAR + FAR) * NT, found)
    eye = lax.broadcasted_iota(jnp.int32, (128, 128), 0) == lax.broadcasted_iota(jnp.int32, (128, 128), 1)
    for n in range(3):
        column_n = jnp.broadcast_to(found[n * 128 : (n + 1) * 128], (128, 128))
        index[n : n + 1, :] = jnp.sum(jnp.where(eye, column_n, 0), axis=0, keepdims=True)
    zero[...] = jnp.zeros_like(zero)

    def update(m, total, weighted, s, v):
        top = jnp.maximum(m, jnp.max(s, axis=1, keepdims=True))
        shrink = jnp.exp(m - top)
        p = jnp.exp(s - top)
        total = total * shrink + jnp.sum(p, axis=1, keepdims=True)
        weighted = weighted * shrink + jnp.dot(p.astype(jnp.bfloat16), v, preferred_element_type=jnp.float32)
        return top, total, weighted

    def dots(a, b):
        return lax.dot_general(a, b, (((1,), (1,)), ((), ())), preferred_element_type=jnp.float32) * scale

    ext_copy.wait()
    ext_out = pltpu.make_async_copy(ext, pages.at[pl.ds(NI * NEAR, FAR)], ext_sem)
    ext_out.start()

    def extra_step(k, carry):
        n = lax.broadcasted_iota(jnp.int32, (1, NT * 64), 1)
        ts = (t + NT - n // 64) % NT
        token = (((NEAR + k) * NT + ts) * NL + l) * 64 + n % 64
        s = dots(qx[...].astype(jnp.bfloat16), ext[k, :, 0].reshape(NT * 64, 128))
        s = jnp.where(token < pos[NI, :, :1], s, MASKED)
        return update(*carry, s, ext[k, :, 1].reshape(NT * 64, 128))

    empty = (
        jnp.full((256, 1), LOW, jnp.float32),
        jnp.zeros((256, 1), jnp.float32),
        jnp.zeros((256, 128), jnp.float32),
    )
    mx, tx, ax = lax.fori_loop(0, FAR, extra_step, empty)

    a = lax.broadcasted_iota(jnp.int32, (256, 16), 0)
    b = lax.broadcasted_iota(jnp.int32, (256, 16), 1)
    visible = (a % 4 == b % 4) & (b // 4 <= (a // 4) % 4) & (l == 0)
    for d in range(NI):
        rows = slice(d * 16, (d + 1) * 16)
        s = jnp.where(visible, dots(q[d], fkv[rows, :128]), MASKED)
        far = jnp.full((256, 1), flag[d]) == 1
        start = (jnp.where(far, mx, LOW), jnp.where(far, tx, 0.0), jnp.where(far, ax, 0.0))
        m, total, weighted = update(*start, s, fkv[rows, 128:])
        acc[d] = weighted
        ml[d, :, :64] = jnp.broadcast_to(m, (256, 64))
        ml[d, :, 64:] = jnp.broadcast_to(total, (256, 64))

    for c in own:
        c.wait()

    def visit(k, c):
        def request(d, c):
            for dt in range(NT):
                if dt:
                    page_copy(k, d, dt).wait_recv()
                else:

                    @pl.when(d != 0)
                    def _():
                        page_copy(k, d, dt).wait_recv()

            pltpu.make_async_copy(recv.at[d, k], pages.at[d * NEAR + k], page_sem.at[d, k]).start()
            n = lax.broadcasted_iota(jnp.int32, (1, NT * 64), 1)
            ts = (t + NT - n // 64) % NT
            token = ((k * NT + ts) * NL + l) * 64 + n % 64
            s = dots(q[d], recv[d, k, :, 0].reshape(NT * 64, 128))
            s = jnp.where(token < pos[d, :, :1], s, MASKED)
            m, total, weighted = update(
                ml[d, :, :1], ml[d, :, 64:65], acc[d], s, recv[d, k, :, 1].reshape(NT * 64, 128)
            )
            acc[d] = weighted
            ml[d, :, :64] = jnp.broadcast_to(m, (256, 64))
            ml[d, :, 64:] = jnp.broadcast_to(total, (256, 64))
            return c

        return lax.fori_loop(0, NI, request, c)

    lax.fori_loop(0, NEAR, visit, 0)

    joins = []
    for dl in range(1, NL):
        to = column(0, dl)
        for part, ref in enumerate((acc, ml)):
            joins.append(
                pltpu.make_async_remote_copy(
                    src_ref=ref.at[to[1]],
                    dst_ref=got.at[dl - 1, part],
                    send_sem=s1_sem.at[dl - 1, part],
                    recv_sem=r1_sem.at[dl - 1, part],
                    device_id=to,
                    device_id_type=MESH,
                )
            )
    for c in joins:
        c.start()
    for c in joins:
        c.wait_recv()
    parts = [(acc[l], ml[l])] + [(got[n, 0], got[n, 1]) for n in range(NL - 1)]
    top = functools.reduce(jnp.maximum, [p[1][:, :1] for p in parts])
    total = sum(p[1][:, 64:65] * jnp.exp(p[1][:, :1] - top) for p in parts)
    weighted = sum(p[0] * jnp.exp(p[1][:, :1] - top) for p in parts)
    joined = (weighted / total).astype(jnp.bfloat16)
    mine = i * NL + l
    for h in range(16):
        ctx[mine, :, h * 128 : (h + 1) * 128] = joined[h * 16 : (h + 1) * 16, :]

    spread = []
    for di in range(NI):
        for dl in range(NL):
            if di or dl:
                spread.append(
                    pltpu.make_async_remote_copy(
                        src_ref=ctx.at[mine],
                        dst_ref=ctx.at[mine],
                        send_sem=s2_sem.at[di, dl],
                        recv_sem=r2_sem.at[di, dl],
                        device_id=column(di, dl),
                        device_id_type=MESH,
                    )
                )
    for c in spread:
        c.start()
    w_copy.wait()
    for c in spread:
        c.wait_recv()
    context = []
    for group in range(NI):
        back = one_hot(places(jnp.int32(group)), across, down)
        rows = ctx[group * NL : (group + 1) * NL].reshape(64, 2048)
        context.append(jnp.dot(back, rows, preferred_element_type=jnp.float32).astype(jnp.bfloat16))
    context = jnp.concatenate(context, axis=0)
    for n in range(NT):
        proj[n] = jnp.dot(context, w[:, n * 128 : (n + 1) * 128], preferred_element_type=jnp.float32)
    sums = []
    for dt in range(1, NT):
        to = plane(0, dt)
        sums.append(
            pltpu.make_async_remote_copy(
                src_ref=proj.at[to[2]],
                dst_ref=red.at[dt - 1],
                send_sem=s4_sem.at[dt - 1],
                recv_sem=r4_sem.at[dt - 1],
                device_id=to,
                device_id_type=MESH,
            )
        )
    for c in sums:
        c.start()

    total = proj[t]
    for n, c in enumerate(sums):
        c.wait_recv()
        total = total + red[n]
    for group in range(NI):
        mine = slice(group * 16, (group + 1) * 16)
        for step in range(4):
            rows = total[group * 64 + step * 16 : group * 64 + (step + 1) * 16]
            attn[step, mine] = rows + residual[step, mine].astype(jnp.float32)

    zero_out = pltpu.make_async_copy(zero, pages.at[NI * NEAR + FAR], own_sem.at[0])
    zero_out.start()
    zero_out.wait()
    ext_out.wait()
    for c in joins + spread + sums:
        c.wait_send()

    def drain(k, c):
        def one(n, c):
            di, dt = pair(n)

            @pl.when(n != 0)
            def _():
                page_copy(k, di, dt).wait_send()

            return c

        for d in range(NI):
            pltpu.make_async_copy(recv.at[d, k], pages.at[d * NEAR + k], page_sem.at[d, k]).wait()
        return lax.fori_loop(0, NI * NT, one, c)

    lax.fori_loop(0, NEAR, drain, 0)


def run_main(*args):
    hbm, vmem, smem = (pl.BlockSpec(memory_space=m) for m in (pl.ANY, pltpu.VMEM, pltpu.SMEM))
    bf, f32, i32, dma = jnp.bfloat16, jnp.float32, jnp.int32, pltpu.SemaphoreType.DMA
    return pl.pallas_call(
        main_kernel,
        out_shape=(
            jax.ShapeDtypeStruct((NI * NEAR + FAR + 1, NT, 2, 64, 128), bf),
            jax.ShapeDtypeStruct((4, 64, 128), f32),
            jax.ShapeDtypeStruct((3, 128), i32),
        ),
        in_specs=[smem] * 5 + [hbm] * 3 + [vmem] * 4,
        out_specs=(hbm, vmem, vmem),
        scratch_shapes=[
            pltpu.VMEM((SRC, 2, NT, 64, 128), bf),
            pltpu.VMEM((NI, NEAR, 2, NT, 64, 128), bf),
            pltpu.VMEM((NI, NEAR, NT, 2, 64, 128), bf),
            pltpu.VMEM((FAR, NT, 2, 64, 128), bf),
            pltpu.VMEM((2048, 1024), bf),
            pltpu.VMEM((NI, 256, 128), bf),
            pltpu.VMEM((256, 128), f32),
            pltpu.VMEM((64, 256), bf),
            pltpu.VMEM((NI + 1, 256, 128), i32),
            pltpu.VMEM((NI, 256, 128), f32),
            pltpu.VMEM((NI, 256, 128), f32),
            pltpu.VMEM((NL - 1, 2, 256, 128), f32),
            pltpu.VMEM((NI * NL, 16, 2048), bf),
            pltpu.VMEM((NT, 256, 128), f32),
            pltpu.VMEM((NT - 1, 256, 128), f32),
            pltpu.VMEM((NT, 2, 64, 128), bf),
            dma((NI, NEAR, NT)),
            dma((NI, NEAR, NT)),
            dma((NEAR,)),
            dma((NI, NEAR)),
            dma,
            dma,
            dma,
            dma((NL - 1, 2)),
            dma((NL - 1, 2)),
            dma((NI, NL)),
            dma((NI, NL)),
            dma((NT - 1,)),
            dma((NT - 1,)),
        ],
        compiler_params=pltpu.CompilerParams(
            collective_id=0, has_side_effects=True, vmem_limit_bytes=56 * 1024 * 1024
        ),
    )(*args)


def place_kernel(index, pages, pool, held, load_sem, sem):
    load = pltpu.make_async_copy(pages, held, load_sem)
    load.start()
    load.wait()

    def place(s, c):
        pltpu.make_async_copy(held.at[index[s // 128, s % 128]], pool.at[s], sem).start()
        return c

    lax.fori_loop(0, SLOTS, place, 0, unroll=8)
    pltpu.make_async_copy(pool, pool, sem).wait()


def place_pages(index, pages):
    smem, hbm = pl.BlockSpec(memory_space=pltpu.SMEM), pl.BlockSpec(memory_space=pl.ANY)
    return pl.pallas_call(
        place_kernel,
        out_shape=jax.ShapeDtypeStruct((SLOTS, 2, 64, 128), jnp.bfloat16),
        in_specs=[smem, hbm],
        out_specs=hbm,
        scratch_shapes=[
            pltpu.VMEM(pages.shape, jnp.bfloat16),
            pltpu.SemaphoreType.DMA,
            pltpu.SemaphoreType.DMA,
        ],
        compiler_params=pltpu.CompilerParams(vmem_limit_bytes=16 * 1024 * 1024),
    )(index, pages)


def shards(
    prefill_pool,
    lengths,
    src_table,
    dst_table,
    row_request,
    positions,
    queries,
    step_key_value,
    out_weight,
    residual,
):
    route = src_table[:, 0] // GROUP * NI + dst_table[:, 0] // GROUP
    extra = lax.switch(
        jnp.sum(jnp.where(lengths == LONGEST, route, 0)),
        [functools.partial(move_extra, p, g) for p in range(NI) for g in range(NI)],
        lengths,
        src_table,
        prefill_pool,
    )
    pages, attn, index = run_main(
        src_table,
        dst_table,
        lengths,
        row_request,
        positions,
        prefill_pool,
        extra,
        out_weight,
        dst_table,
        queries.reshape(64, 2048),
        step_key_value.reshape(64, 256),
        residual,
    )
    pool = place_pages(index, pages.reshape((NI * NEAR + FAR + 1) * NT, 2, 64, 128))
    return pool.reshape(SLOTS, 2, 1, 64, 128), attn


def solution(mesh):
    in_specs = (
        P(("instance", "layout", "tensor"), None, None, None, None),
        P(),
        P(),
        P(),
        P(),
        P(),
        P(None, "instance", "tensor"),
        P(None, "instance", None, "tensor", None),
        P("tensor", ("instance", "layout")),
        P(None, None, ("instance", "layout", "tensor")),
    )
    out_specs = (
        P(("instance", "layout"), None, "tensor", None, None),
        P(None, None, ("instance", "layout", "tensor")),
    )
    return jax.shard_map(shards, mesh=mesh, in_specs=in_specs, out_specs=out_specs, check_vma=False)
```

time: 243 us -> 191 us (0.79)
  local copies, waits for them, and re-layouts: 32.9 us -> 6.31 us
  Pallas kernels: 196 us -> 178 us
  other arithmetic: 9.91 us -> 2.97 us
    gather x3 -> x0, local copies, waits for them, and re-layouts: 27 us -> none  [the longest x1 14 us: shards(): pool = pages.reshape((NI * NEAR + FAR + 1) * NT, 2, 64, 128)[index]]
    pallas_call x1, Pallas kernels: 193 us -> 170 us  [run_main(): pl.pallas_call(main_kernel, out_shape=(jax.ShapeDtypeStruct((NI * NEAR +...]
    pallas_call x0 -> x1, Pallas kernels: none -> 4.67 us  [place_pages(): pl.pallas_call(place_kernel, out_shape=jax.ShapeDtypeStruct((SLOTS, 2, 64...]
    reduce_sum x10 -> x1, other arithmetic: 4.43 us -> 1.3 us  [shards(): jnp.sum(jnp.where(lengths == LONGEST, route, 0))]
    unnamed x15 -> x8, local copies, waits for them, and re-layouts: 3.94 us -> 6.31 us
where the time goes in v2:
time: 191 us; the launch traced here: 190 us
  Pallas kernels  178 us (93%)
  local copies, waits for them, and re-layouts  6.31 us (3%)
  other arithmetic  2.97 us (2%)
    pallas_call x1, Pallas kernels, run_main(): pl.pallas_call(main_kernel, out_shape=(jax.ShapeDtypeStruct((NI * NEAR +...  170 us
    unnamed x8, local copies, waits for them, and re-layouts  6.31 us
    pallas_call x1, Pallas kernels, place_pages(): pl.pallas_call(place_kernel, out_shape=jax.ShapeDtypeStruct((SLOTS, 2, 64...  4.67 us

profile of v2, /device:TPU:1, one launch (start us, length us, event | category | flops | bytes accessed | tf_op | source)
XLA Modules:
  0.0 190.4 jit_solution(2477134586909501212)
XLA Ops:
  0.6 0.8 divide_reduce_fusion
  1.5 0.8 fusion.2
  2.3 1.3 fusion.6
  4.3 1.4 copy.16
  5.6 5.1 %conditional.1 = (bf16[10,8,2,64,128]{4,3,2,1,0:T(8,128)(2,1)S(1)}) conditional(s32[]{:T(128)} %clamp.3, (s32[16]{0:T(128)}, s32[16,512]{1,0:T(8,128)}, bf16[36,2,8,64,128]{4,3,2,1,0:T(8,128)(2,1)}) %tuple.56, (s32[16]{0:T(128)}, s32[16,512]{1,0:T(8,128)}, bf16[36,2,8,64,128]{4,3,2,1,0:T(8,128)(2,1)}) %tuple.56, ...), branch_computations={%region_1.2_spmd, %region_2.3_spmd, %region_3.4_spmd, %region_4.5_... | conditional | bytes 8 | solution.py:643
  5.6 3.4 %branch_10_fun.1 = bf16[10,8,2,64,128]{4,3,2,1,0:T(8,128)(2,1)S(1)} custom-call(s32[16]{0:T(128)} %get-tuple-element.143.lengths, s32[16,512]{1,0:T(8,128)} %get-tuple-element.144.table, bf16[36,2,8,64,128]{4,3,2,1,0:T(8,128)(2,1)} %get-tuple-element.145.pool), custom_call_target="tpu_custom_call" | custom-call | tf_op jit(solution)/shard_map/cond/branch_10_fun/pallas_call | solution.py:175
  10.7 170.1 %shard_map.113 = (bf16[35,8,2,64,128]{4,3,2,1,0:T(8,128)(2,1)}, f32[4,64,128]{2,1,0:T(8,128)}, s32[3,128]{1,0:T(4,128)}) custom-call(s32[16,512]{1,0:T(8,128)} %table.1, s32[16,512]{1,0:T(8,128)} %target_v.1, s32[16]{0:T(128)} %lengths.1, s32[64]{0:T(128)} %row_request.1, s32[64]{0:T(128)} %positions.1, bf16[36,2,8,64,128]{4,3,2,1,0:T(8,128)(2,1)} %pool.1, ...), custom_call_target="tpu_custom_call" | custom-call | tf_op jit(solution)/shard_map/pallas_call | solution.py:555
  180.8 0.0 copy-start
  180.8 3.6 %copy-done = bf16[35,8,2,64,128]{4,3,2,1,0:T(8,128)(2,1)S(1)} copy-done((bf16[35,8,2,64,128]{4,3,2,1,0:T(8,128)(2,1)S(1)}, bf16[35,8,2,64,128]{4,3,2,1,0:T(8,128)(2,1)}, u32[]{:S(2)}) %copy-start) | copy-done | bytes 9175064
  184.4 0.0 copy-start.1
  184.4 0.7 copy-done.1
  185.1 0.0 copy-start.2
  185.1 4.7 %shard_map.114 = bf16[288,2,64,128]{3,2,1,0:T(8,128)(2,1)} custom-call(s32[3,128]{1,0:T(4,128)S(1)} %copy-done.1, bf16[280,2,64,128]{3,2,1,0:T(8,128)(2,1)S(1)} %bitcast.11), custom_call_target="tpu_custom_call" | custom-call | tf_op jit(solution)/shard_map/pallas_call | solution.py:616
  189.7 0.0 copy-done.2
  189.8 0.7 copy.34
Async XLA Ops:
  180.8 3.6 %copy-start = (bf16[35,8,2,64,128]{4,3,2,1,0:T(8,128)(2,1)S(1)}, bf16[35,8,2,64,128]{4,3,2,1,0:T(8,128)(2,1)}, u32[]{:S(2)}) copy-start(bf16[35,8,2,64,128]{4,3,2,1,0:T(8,128)(2,1)} %get-tuple-element.167) | copy-start | bytes 27525124
  184.4 0.7 copy-start.1
  185.1 4.7 %copy-start.2 = (f32[4,64,128]{2,1,0:T(8,128)S(1)}, f32[4,64,128]{2,1,0:T(8,128)}, u32[]{:S(2)}) copy-start(f32[4,64,128]{2,1,0:T(8,128)} %get-tuple-element.180) | copy-start | bytes 393220

commit v3 on v2

--- a/solution.py
+++ b/solution.py
@@ -12,6 +12,9 @@
 MASKED = -2e30
 NI, NL, NT = 4, 4, 8
 NEAR = 6
+PARTS = 4
+HEADS = NT // PARTS
+AHEAD = 3
 FAR = 10
 LONGEST = 32768
 SRC = 36
@@ -25,7 +28,7 @@
         return [(0, FAR, [])]
     if way == 2:
         return [(0, FAR // 2, [(p + 1) % NI]), (FAR // 2, FAR, [(p - 1) % NI])]
-    return [(0, 6, []), (6, FAR, [(p - way) % NI, (p - 2 * way) % NI])]
+    return [(0, FAR // 2, []), (FAR // 2, FAR, [(p - way) % NI, (p - 2 * way) % NI])]
 
 
 def find(lengths):
@@ -36,12 +39,12 @@
     i, l, t = (lax.axis_index(a) for a in ("instance", "layout", "tensor"))
     barrier = pltpu.get_barrier_semaphore()
 
-    def hop_copy(k, half, src, to):
+    def hop_copy(k, part, src, to):
         return pltpu.make_async_remote_copy(
             src_ref=src,
-            dst_ref=hop.at[k, half],
-            send_sem=hop_send.at[k, half],
-            recv_sem=hop_recv.at[k, half],
+            dst_ref=hop.at[k, part],
+            send_sem=hop_send.at[k, part],
+            recv_sem=hop_recv.at[k, part],
             device_id=(to, l, t),
             device_id_type=MESH,
         )
@@ -87,21 +90,24 @@
             slot = table[request, ((NEAR + k) * NT + t) * NL + l] - rank * SRC
             packed[k] = held[jnp.clip(slot, 0, SRC - 1)]
 
-        def direct(k, c):
-            pack(k)
-            for dt in range(first, NT):
-                head = lax.rem(t + dt, NT)
-                last_copy(k, head, packed.at[k, :, head]).start()
+        def send(k, c):
+            for lo, hi, via in reversed(routes(p, g)):
+
+                @pl.when(lo + k < hi)
+                def _():
+                    pack(lo + k)
+                    if via:
+                        for part in range(PARTS):
+                            src = packed.at[lo + k, :, part * HEADS : (part + 1) * HEADS]
+                            hop_copy(lo + k, part, src, via[0]).start()
+                    else:
+                        for dt in range(first, NT):
+                            head = lax.rem(t + dt, NT)
+                            last_copy(lo + k, head, packed.at[lo + k, :, head]).start()
+
             return c
 
-        def relayed(to, k, c):
-            pack(k)
-            for half in range(2):
-                hop_copy(k, half, packed.at[k, :, half * 4 : half * 4 + 4], to).start()
-            return c
-
-        for lo, hi, via in reversed(routes(p, g)):
-            lax.fori_loop(lo, hi, functools.partial(relayed, via[0]) if via else direct, 0)
+        lax.fori_loop(0, max(hi - lo for lo, hi, _ in routes(p, g)), send, 0)
 
     for lo, hi, via in routes(p, g):
         for n, node in enumerate(via):
@@ -111,14 +117,14 @@
                 pl.semaphore_wait(barrier, 1 if n + 1 < len(via) else NT)
 
                 def forward(k, c):
-                    for half in range(2):
-                        hop_copy(k, half, hop.at[k, half], node).wait_recv()
+                    for part in range(PARTS):
+                        hop_copy(k, part, hop.at[k, part], node).wait_recv()
                         if n + 1 < len(via):
-                            hop_copy(k, half, hop.at[k, half], via[n + 1]).start()
+                            hop_copy(k, part, hop.at[k, part], via[n + 1]).start()
                         else:
-                            for hh in range(4):
-                                h = lax.rem(t + hh, 4)
-                                last_copy(k, half * 4 + h, hop.at[k, half, :, h]).start()
+                            for hh in range(HEADS):
+                                h = lax.rem(t + hh, HEADS)
+                                last_copy(k, part * HEADS + h, hop.at[k, part, :, h]).start()
                     return c
 
                 lax.fori_loop(lo, hi, forward, 0)
@@ -148,8 +154,8 @@
             def _():
                 def drain(k, c):
                     if n + 1 < len(nodes):
-                        for half in range(2):
-                            hop_copy(k, half, hop.at[k, half], node).wait_send()
+                        for part in range(PARTS):
+                            hop_copy(k, part, hop.at[k, part], node).wait_send()
                     else:
                         for dt in range(first, NT):
                             head = lax.rem(t + dt, NT)
@@ -180,12 +186,12 @@
         scratch_shapes=[
             pltpu.VMEM((SRC, 2, NT, 64, 128), bf),
             pltpu.VMEM((FAR, 2, NT, 64, 128), bf),
-            pltpu.VMEM((FAR, 2, 2, 4, 64, 128), bf),
+            pltpu.VMEM((FAR, PARTS, 2, HEADS, 64, 128), bf),
             pltpu.VMEM((NT, 2, 64, 128), bf),
             dma((NT, FAR)),
             dma((NT, FAR)),
-            dma((FAR, 2)),
-            dma((FAR, 2)),
+            dma((FAR, PARTS)),
+            dma((FAR, PARTS)),
             dma((FAR,)),
         ],
         compiler_params=pltpu.CompilerParams(
@@ -221,6 +227,9 @@
     pos,
     acc,
     ml,
+    back,
+    reqs,
+    give,
     got,
     ctx,
     proj,
@@ -263,7 +272,9 @@
     w_copy = pltpu.make_async_copy(weight, w, w_sem)
     ext_copy = pltpu.make_async_copy(extra, ext, ext_sem)
     ext_copy.start()
-    own = [pltpu.make_async_copy(send.at[0, k, :, t], recv.at[0, k, 0], own_sem.at[k]) for k in range(NEAR)]
+
+    def own_copy(k):
+        return pltpu.make_async_copy(send.at[0, k, :, t], recv.at[0, k, 0], own_sem.at[k])
 
     out_req = [jnp.int32(0)] * NI
     in_req = [jnp.int32(0)] * NI
@@ -272,7 +283,9 @@
         for d in range(NI):
             out_req[d] = jnp.where((src_r == i) & (dst_r == lax.rem(i + d, NI)), r, out_req[d])
             in_req[d] = jnp.where((dst_r == i) & (src_r == lax.rem(i + NI - d, NI)), r, in_req[d])
-    rank = (i * NL + l) * NT + t
+    for d in range(NI):
+        reqs[d] = out_req[d]
+    base = ((i * NL + l) * NT + t) * SRC
     pl.semaphore_wait(barrier, NI * NT - 1 + NI * (NL - 1))
     load.wait()
 
@@ -287,32 +300,38 @@
             device_id_type=MESH,
         )
 
-    def pair(n):
-        di = n % 4
-        dz = (di + n // 8) % 4
-        return di, dz * 2 + (n // 4) % 2
-
-    def send_page(k, c):
-        for d in range(NI):
-            slot = table[out_req[d], (k * NT + t) * NL + l] - rank * SRC
+    def pair(n, m):
+        d = n // NEAR + 2 * ((m // 2) % 2)
+        return d, ((d + m // 4) % 4) * 2 + m % 2
+
+    def each(n, act):
+        def one(m, c):
+            d, dt = pair(n, m)
+
+            @pl.when((d != 0) | (dt != 0))
+            def _():
+                act(page_copy(n % NEAR, d, dt))
+
+            return c
+
+        lax.fori_loop(0, 16, one, 0)
+
+    def issue(n, c):
+        k = n % NEAR
+        for half in range(2):
+            d = n // NEAR + 2 * half
+            slot = table[reqs[d], (k * NT + t) * NL + l] - base
             send[d, k] = held[jnp.clip(slot, 0, SRC - 1)]
-
-        def one(n, c):
-            di, dt = pair(n)
-
-            @pl.when(n != 0)
-            def _():
-                page_copy(k, di, dt).start()
-
-            return c
-
-        return lax.fori_loop(0, NI * NT, one, c)
-
-    lax.fori_loop(0, NEAR, send_page, 0)
+        each(n, lambda c: c.start())
+
+        @pl.when(n < NEAR)
+        def _():
+            own_copy(k).start()
+
+        return c
+
+    lax.fori_loop(0, AHEAD, issue, 0)
     w_copy.start()
-
-    for c in own:
-        c.start()
 
     def places(group):
         count, found = [jnp.int32(0)] * NI, []
@@ -335,6 +354,9 @@
     across = lax.broadcasted_iota(jnp.int32, (64, 64), 1)
     here = places(i)
     pick = one_hot(here, down, across)
+
+    for group in range(NI):
+        back[group] = one_hot(places(jnp.int32(group)), across, down)
 
     sorted_q = jnp.dot(pick, query[...], preferred_element_type=jnp.float32).astype(jnp.bfloat16)
     fkv[...] = jnp.dot(pick, fresh[...], preferred_element_type=jnp.float32).astype(jnp.bfloat16)
@@ -413,24 +435,24 @@
         ml[d, :, :64] = jnp.broadcast_to(m, (256, 64))
         ml[d, :, 64:] = jnp.broadcast_to(total, (256, 64))
 
-    for c in own:
-        c.wait()
-
-    def visit(k, c):
-        def request(d, c):
-            for dt in range(NT):
-                if dt:
-                    page_copy(k, d, dt).wait_recv()
-                else:
-
-                    @pl.when(d != 0)
-                    def _():
-                        page_copy(k, d, dt).wait_recv()
-
+    def visit(n, c):
+        k = n % NEAR
+        each(n, lambda c: c.wait_recv())
+
+        @pl.when(n < NEAR)
+        def _():
+            own_copy(k).wait()
+
+        @pl.when(n + AHEAD < 2 * NEAR)
+        def _():
+            issue(n + AHEAD, 0)
+
+        def request(half, c):
+            d = n // NEAR + 2 * half
             pltpu.make_async_copy(recv.at[d, k], pages.at[d * NEAR + k], page_sem.at[d, k]).start()
-            n = lax.broadcasted_iota(jnp.int32, (1, NT * 64), 1)
-            ts = (t + NT - n // 64) % NT
-            token = ((k * NT + ts) * NL + l) * 64 + n % 64
+            column = lax.broadcasted_iota(jnp.int32, (1, NT * 64), 1)
+            ts = (t + NT - column // 64) % NT
+            token = ((k * NT + ts) * NL + l) * 64 + column % 64
             s = dots(q[d], recv[d, k, :, 0].reshape(NT * 64, 128))
             s = jnp.where(token < pos[d, :, :1], s, MASKED)
             m, total, weighted = update(
@@ -441,112 +463,180 @@
             ml[d, :, 64:] = jnp.broadcast_to(total, (256, 64))
             return c
 
-        return lax.fori_loop(0, NI, request, c)
-
-    lax.fori_loop(0, NEAR, visit, 0)
-
-    joins = []
-    for dl in range(1, NL):
-        to = column(0, dl)
-        for part, ref in enumerate((acc, ml)):
-            joins.append(
+        return lax.fori_loop(0, 2, request, c)
+
+    eye = lax.broadcasted_iota(jnp.int32, (64, 128), 0) == lax.broadcasted_iota(jnp.int32, (64, 128), 1)
+
+    def send_parts(stage):
+        for half in range(2):
+            d = stage + 2 * half
+            for n in range(NL):
+                rows = slice(n * 64, (n + 1) * 64)
+                give[stage, n, half * 64 : (half + 1) * 64, :] = acc[d, rows, :]
+                for part in range(2):
+                    stat = jnp.where(eye, ml[d, rows, part * 64 : part * 64 + 1], 0.0)
+                    row = 128 + half * 2 + part
+                    give[stage, n, row : row + 1, :] = jnp.sum(stat, axis=0, keepdims=True)
+        copies = []
+        for dl in range(1, NL):
+            to = column(0, dl)
+            copies.append(
                 pltpu.make_async_remote_copy(
-                    src_ref=ref.at[to[1]],
-                    dst_ref=got.at[dl - 1, part],
-                    send_sem=s1_sem.at[dl - 1, part],
-                    recv_sem=r1_sem.at[dl - 1, part],
+                    src_ref=give.at[stage, to[1]],
+                    dst_ref=got.at[stage, dl - 1],
+                    send_sem=s1_sem.at[stage, dl - 1],
+                    recv_sem=r1_sem.at[stage, dl - 1],
                     device_id=to,
                     device_id_type=MESH,
                 )
             )
-    for c in joins:
-        c.start()
-    for c in joins:
-        c.wait_recv()
-    parts = [(acc[l], ml[l])] + [(got[n, 0], got[n, 1]) for n in range(NL - 1)]
-    top = functools.reduce(jnp.maximum, [p[1][:, :1] for p in parts])
-    total = sum(p[1][:, 64:65] * jnp.exp(p[1][:, :1] - top) for p in parts)
-    weighted = sum(p[0] * jnp.exp(p[1][:, :1] - top) for p in parts)
-    joined = (weighted / total).astype(jnp.bfloat16)
-    mine = i * NL + l
-    for h in range(16):
-        ctx[mine, :, h * 128 : (h + 1) * 128] = joined[h * 16 : (h + 1) * 16, :]
-
-    spread = []
-    for di in range(NI):
-        for dl in range(NL):
-            if di or dl:
-                spread.append(
-                    pltpu.make_async_remote_copy(
-                        src_ref=ctx.at[mine],
-                        dst_ref=ctx.at[mine],
-                        send_sem=s2_sem.at[di, dl],
-                        recv_sem=r2_sem.at[di, dl],
-                        device_id=column(di, dl),
-                        device_id_type=MESH,
-                    )
+        for c in copies:
+            c.start()
+        return copies
+
+    def by_x(stage, half):
+        return stage == 0 or half == 0
+
+    def spread(stage, half, phase, rows):
+        along_x = by_x(stage, half) == (phase == 0)
+        copies = []
+        for n in range(1, NI):
+            copies.append(
+                pltpu.make_async_remote_copy(
+                    src_ref=rows,
+                    dst_ref=rows,
+                    send_sem=s2_sem.at[stage, half, phase, n],
+                    recv_sem=r2_sem.at[stage, half, phase, n],
+                    device_id=column(n, 0) if along_x else column(0, n),
+                    device_id_type=MESH,
                 )
-    for c in spread:
-        c.start()
+            )
+        for c in copies:
+            c.start()
+        return copies
+
+
+    def join(stage, copies):
+        for c in copies:
+            c.wait_recv()
+        sent = []
+        blocks = [give.at[stage, l]] + [got.at[stage, n] for n in range(NL - 1)]
+        for half in range(2):
+
+            def stat(block, part):
+                row = 128 + half * 2 + part
+                return jnp.sum(jnp.where(eye, block[row : row + 1, :], 0.0), axis=1, keepdims=True)
+
+            tops = [stat(block, 0) for block in blocks]
+            top = functools.reduce(jnp.maximum, tops)
+            shares = [jnp.exp(x - top) for x in tops]
+            total = sum(stat(block, 1) * share for block, share in zip(blocks, shares))
+            weighted = sum(block[half * 64 : (half + 1) * 64, :] * share for block, share in zip(blocks, shares))
+            joined = (weighted / total).astype(jnp.bfloat16)
+            mine = l * NI + i if by_x(stage, half) else i * NL + l
+            for h in range(4):
+                ctx[stage, half, mine, :, h * 128 : (h + 1) * 128] = joined[h * 16 : (h + 1) * 16]
+            sent.append(spread(stage, half, 0, ctx.at[stage, half, mine]))
+        return sent
+
+    def widen(stage, sent):
+        wide = []
+        for half in range(2):
+            for c in sent[half]:
+                c.wait_recv()
+            at = l * NI if by_x(stage, half) else i * NL
+            wide.append(spread(stage, half, 1, ctx.at[stage, half, pl.ds(at, NI)]))
+        return wide
+
+    def project(stage, wide):
+        for c in wide[0] + wide[1]:
+            c.wait_recv()
+
+        def block(group, half, n):
+            return ctx[stage, half, n * NI + group if by_x(stage, half) else group * NL + n]
+
+        context = jnp.concatenate(
+            [
+                jnp.concatenate([block(group, half, n) for n in range(NL)], axis=1)
+                for group in range(NI)
+                for half in range(2)
+            ],
+            axis=0,
+        )
+        for n in range(NT // 2):
+            out = jnp.dot(context, w[:, n * 256 : (n + 1) * 256], preferred_element_type=jnp.float32)
+            proj[stage, 2 * n] = out[:, :128]
+            proj[stage, 2 * n + 1] = out[:, 128:]
+        copies = []
+        for dt in range(1, NT):
+            to = plane(0, dt)
+            copies.append(
+                pltpu.make_async_remote_copy(
+                    src_ref=proj.at[stage, to[2]],
+                    dst_ref=red.at[stage, dt - 1],
+                    send_sem=s4_sem.at[stage, dt - 1],
+                    recv_sem=r4_sem.at[stage, dt - 1],
+                    device_id=to,
+                    device_id_type=MESH,
+                )
+            )
+        for c in copies:
+            c.start()
+        return copies
+
+    def reduce(stage, copies):
+        total = proj[stage, t]
+        for n, c in enumerate(copies):
+            c.wait_recv()
+            total = total + red[stage, n]
+        return total
+
+    lax.fori_loop(0, 6, visit, 0)
+    parts = [send_parts(0)]
+    lax.fori_loop(6, 7, visit, 0)
+    contexts = join(0, parts[0])
+    lax.fori_loop(7, 8, visit, 0)
+    wide = widen(0, contexts)
+    contexts += wide
+    lax.fori_loop(8, 10, visit, 0)
     w_copy.wait()
-    for c in spread:
-        c.wait_recv()
-    context = []
+    sums = [project(0, wide)]
+    lax.fori_loop(10, 12, visit, 0)
+    parts.append(send_parts(1))
+    first = reduce(0, sums[0])
+    sent = join(1, parts[1])
+    wide = widen(1, sent)
+    contexts += sent + wide
+    sums.append(project(1, wide))
+    second = reduce(1, sums[1])
+
     for group in range(NI):
-        back = one_hot(places(jnp.int32(group)), across, down)
-        rows = ctx[group * NL : (group + 1) * NL].reshape(64, 2048)
-        context.append(jnp.dot(back, rows, preferred_element_type=jnp.float32).astype(jnp.bfloat16))
-    context = jnp.concatenate(context, axis=0)
-    for n in range(NT):
-        proj[n] = jnp.dot(context, w[:, n * 128 : (n + 1) * 128], preferred_element_type=jnp.float32)
-    sums = []
-    for dt in range(1, NT):
-        to = plane(0, dt)
-        sums.append(
-            pltpu.make_async_remote_copy(
-                src_ref=proj.at[to[2]],
-                dst_ref=red.at[dt - 1],
-                send_sem=s4_sem.at[dt - 1],
-                recv_sem=r4_sem.at[dt - 1],
-                device_id=to,
-                device_id_type=MESH,
-            )
-        )
-    for c in sums:
-        c.start()
-
-    total = proj[t]
-    for n, c in enumerate(sums):
-        c.wait_recv()
-        total = total + red[n]
-    for group in range(NI):
-        mine = slice(group * 16, (group + 1) * 16)
+        value = jnp.concatenate([(first, second)[d % 2][group * 32 + d // 2 * 16 :][:16] for d in range(NI)], axis=0)
+        ordered = jnp.zeros((64, 128), jnp.float32)
+        for _ in range(3):
+            piece = value.astype(jnp.bfloat16)
+            value = value - piece.astype(jnp.float32)
+            ordered += jnp.dot(back[group], piece, preferred_element_type=jnp.float32)
+        own_rows = slice(group * 16, (group + 1) * 16)
         for step in range(4):
-            rows = total[group * 64 + step * 16 : group * 64 + (step + 1) * 16]
-            attn[step, mine] = rows + residual[step, mine].astype(jnp.float32)
+            attn[step, own_rows] = ordered[step * 16 : (step + 1) * 16] + residual[step, own_rows].astype(jnp.float32)
 
     zero_out = pltpu.make_async_copy(zero, pages.at[NI * NEAR + FAR], own_sem.at[0])
     zero_out.start()
     zero_out.wait()
     ext_out.wait()
-    for c in joins + spread + sums:
-        c.wait_send()
-
-    def drain(k, c):
-        def one(n, c):
-            di, dt = pair(n)
-
-            @pl.when(n != 0)
-            def _():
-                page_copy(k, di, dt).wait_send()
-
-            return c
-
-        for d in range(NI):
-            pltpu.make_async_copy(recv.at[d, k], pages.at[d * NEAR + k], page_sem.at[d, k]).wait()
-        return lax.fori_loop(0, NI * NT, one, c)
-
-    lax.fori_loop(0, NEAR, drain, 0)
+    for copies in parts + contexts + sums:
+        for c in copies:
+            c.wait_send()
+
+    def drain(n, c):
+        each(n, lambda c: c.wait_send())
+        for half in range(2):
+            d = n // NEAR + 2 * half
+            pltpu.make_async_copy(recv.at[d, n % NEAR], pages.at[d * NEAR + n % NEAR], page_sem.at[d, n % NEAR]).wait()
+        return c
+
+    lax.fori_loop(0, 2 * NEAR, drain, 0)
 
 
 def run_main(*args):
@@ -559,7 +649,7 @@
             jax.ShapeDtypeStruct((4, 64, 128), f32),
             jax.ShapeDtypeStruct((3, 128), i32),
         ),
-        in_specs=[smem] * 5 + [hbm] * 3 + [vmem] * 4,
+        in_specs=[smem] * 5 + [hbm, hbm, pl.BlockSpec(memory_space=pltpu.HBM)] + [vmem] * 4,
         out_specs=(hbm, vmem, vmem),
         scratch_shapes=[
             pltpu.VMEM((SRC, 2, NT, 64, 128), bf),
@@ -573,10 +663,13 @@
             pltpu.VMEM((NI + 1, 256, 128), i32),
             pltpu.VMEM((NI, 256, 128), f32),
             pltpu.VMEM((NI, 256, 128), f32),
-            pltpu.VMEM((NL - 1, 2, 256, 128), f32),
-            pltpu.VMEM((NI * NL, 16, 2048), bf),
-            pltpu.VMEM((NT, 256, 128), f32),
-            pltpu.VMEM((NT - 1, 256, 128), f32),
+            pltpu.VMEM((NI, 64, 64), bf),
+            pltpu.SMEM((NI,), i32),
+            pltpu.VMEM((2, NL, 136, 128), f32),
+            pltpu.VMEM((2, NL - 1, 136, 128), f32),
+            pltpu.VMEM((2, 2, NI * NL, 16, 512), bf),
+            pltpu.VMEM((2, NT, 128, 128), f32),
+            pltpu.VMEM((2, NT - 1, 128, 128), f32),
             pltpu.VMEM((NT, 2, 64, 128), bf),
             dma((NI, NEAR, NT)),
             dma((NI, NEAR, NT)),
@@ -585,26 +678,22 @@
             dma,
             dma,
             dma,
-            dma((NL - 1, 2)),
-            dma((NL - 1, 2)),
-            dma((NI, NL)),
-            dma((NI, NL)),
-            dma((NT - 1,)),
-            dma((NT - 1,)),
+            dma((2, NL - 1)),
+            dma((2, NL - 1)),
+            dma((2, 2, 2, NI)),
+            dma((2, 2, 2, NI)),
+            dma((2, NT - 1)),
+            dma((2, NT - 1)),
         ],
         compiler_params=pltpu.CompilerParams(
-            collective_id=0, has_side_effects=True, vmem_limit_bytes=56 * 1024 * 1024
+            collective_id=0, has_side_effects=True, vmem_limit_bytes=40 * 1024 * 1024
         ),
     )(*args)
 
 
-def place_kernel(index, pages, pool, held, load_sem, sem):
-    load = pltpu.make_async_copy(pages, held, load_sem)
-    load.start()
-    load.wait()
-
+def place_kernel(index, pages, pool, sem):
     def place(s, c):
-        pltpu.make_async_copy(held.at[index[s // 128, s % 128]], pool.at[s], sem).start()
+        pltpu.make_async_copy(pages.at[index[s // 128, s % 128]], pool.at[s], sem).start()
         return c
 
     lax.fori_loop(0, SLOTS, place, 0, unroll=8)
@@ -618,12 +707,8 @@
         out_shape=jax.ShapeDtypeStruct((SLOTS, 2, 64, 128), jnp.bfloat16),
         in_specs=[smem, hbm],
         out_specs=hbm,
-        scratch_shapes=[
-            pltpu.VMEM(pages.shape, jnp.bfloat16),
-            pltpu.SemaphoreType.DMA,
-            pltpu.SemaphoreType.DMA,
-        ],
-        compiler_params=pltpu.CompilerParams(vmem_limit_bytes=16 * 1024 * 1024),
+        scratch_shapes=[pltpu.SemaphoreType.DMA],
+        compiler_params=pltpu.CompilerParams(vmem_limit_bytes=12 * 1024 * 1024),
     )(index, pages)
 
 
@@ -639,7 +724,8 @@
     out_weight,
     residual,
 ):
-    route = src_table[:, 0] // GROUP * NI + dst_table[:, 0] // GROUP
+    src, dst = src_table[:, 0], dst_table[:, 0]
+    route = sum((src >= n * GROUP).astype(jnp.int32) * NI + (dst >= n * GROUP).astype(jnp.int32) for n in range(1, NI))
     extra = lax.switch(
         jnp.sum(jnp.where(lengths == LONGEST, route, 0)),
         [functools.partial(move_extra, p, g) for p in range(NI) for g in range(NI)],

time: 191 us -> 178 us (0.932)
  Pallas kernels: 178 us -> 170 us
  local copies, waits for them, and re-layouts: 6.31 us -> 3.63 us
    pallas_call x1, Pallas kernels: 170 us -> 122 us  [run_main(): pl.pallas_call(main_kernel, out_shape=(jax.ShapeDtypeStruct((NI * NEAR +...]
    pallas_call x1, Pallas kernels: 3.36 us -> 44.5 us  [move_extra(): pl.pallas_call(functools.partial(extra_kernel, p, g), out_shape=jax.Shape...]
    unnamed x8 -> x14, local copies, waits for them, and re-layouts: 6.31 us -> 3.63 us
where the time goes in v3:
time: 178 us
  Pallas kernels  170 us (96%)
  local copies, waits for them, and re-layouts  3.63 us (2%)
  other arithmetic  2.13 us (1%)
    pallas_call x1, Pallas kernels, run_main(): pl.pallas_call(main_kernel, out_shape=(jax.ShapeDtypeStruct((NI * NEAR +...  122 us
    pallas_call x1, Pallas kernels, move_extra(): pl.pallas_call(functools.partial(extra_kernel, p, g), out_shape=jax.Shape...  44.5 us
    pallas_call x1, Pallas kernels, place_pages(): pl.pallas_call(place_kernel, out_shape=jax.ShapeDtypeStruct((SLOTS, 2, 64...  4.06 us
    unnamed x14, local copies, waits for them, and re-layouts  3.63 us

profile of v3, /device:TPU:1, one launch (start us, length us, event | category | flops | bytes accessed | tf_op | source)
XLA Modules:
  0.0 177.7 jit_solution(14306669913382131933)
XLA Ops:
  0.6 0.8 add_reduce_fusion
  1.5 1.3 fusion
  3.4 0.8 copy.16
  4.2 0.0 copy-start.1
  4.2 0.0 copy-start.2
  4.2 0.0 copy-start.3
  4.2 0.0 copy-start.4
  4.2 0.0 copy-start.5
  4.2 45.0 %conditional.1 = (bf16[10,8,2,64,128]{4,3,2,1,0:T(8,128)(2,1)S(1)}) conditional(s32[]{:T(128)} %clamp.3, (s32[16]{0:T(128)}, s32[16,512]{1,0:T(8,128)}, bf16[36,2,8,64,128]{4,3,2,1,0:T(8,128)(2,1)}) %tuple.56, (s32[16]{0:T(128)}, s32[16,512]{1,0:T(8,128)}, bf16[36,2,8,64,128]{4,3,2,1,0:T(8,128)(2,1)}) %tuple.56, ...), branch_computations={%region_1.2_spmd, %region_2.3_spmd, %region_3.4_spmd, %region_4.5_... | conditional | bytes 8 | solution.py:729
  4.5 44.5 %branch_11_fun.1 = bf16[10,8,2,64,128]{4,3,2,1,0:T(8,128)(2,1)S(1)} custom-call(s32[16]{0:T(128)} %get-tuple-element.146.lengths, s32[16,512]{1,0:T(8,128)} %get-tuple-element.147.table, bf16[36,2,8,64,128]{4,3,2,1,0:T(8,128)(2,1)} %get-tuple-element.148.pool), custom_call_target="tpu_custom_call" | custom-call | tf_op jit(solution)/shard_map/cond/branch_11_fun/pallas_call | solution.py:181
  49.2 0.0 copy-done.1
  49.3 0.0 copy-done.2
  49.3 0.0 copy-done.3
  49.3 0.0 copy-done.4
  49.3 0.0 copy-done.5
  49.3 0.0 copy-start
  49.3 2.2 %copy-done = bf16[2048,1024]{1,0:T(8,128)(2,1)S(1)} copy-done((bf16[2048,1024]{1,0:T(8,128)(2,1)S(1)}, bf16[2048,1024]{1,0:T(8,128)(2,1)}, u32[]{:S(2)}) %copy-start) | copy-done | bytes 4194328
  51.5 121.5 %shard_map.113 = (bf16[35,8,2,64,128]{4,3,2,1,0:T(8,128)(2,1)S(1)}, f32[4,64,128]{2,1,0:T(8,128)S(1)}, s32[3,128]{1,0:T(4,128)S(1)}) custom-call(s32[16,512]{1,0:T(8,128)} %table.1, s32[16,512]{1,0:T(8,128)S(1)} %copy-done.2, s32[16]{0:T(128)} %lengths.1, s32[64]{0:T(128)S(1)} %copy-done.4, s32[64]{0:T(128)S(1)} %copy-done.5, ...), custom_call_target="tpu_custom_call" | custom-call | tf_op jit(solution)/shard_map/pallas_call | solution.py:645
  173.0 4.1 %shard_map.114 = bf16[288,2,64,128]{3,2,1,0:T(8,128)(2,1)} custom-call(s32[3,128]{1,0:T(4,128)S(1)} %get-tuple-element.166.index, bf16[280,2,64,128]{3,2,1,0:T(8,128)(2,1)S(1)} %bitcast.11), custom_call_target="tpu_custom_call" | custom-call | tf_op jit(solution)/shard_map/pallas_call | solution.py:705
  177.1 0.7 copy.34
Async XLA Ops:
  4.2 45.1 %copy-start.1 = (bf16[4,16,2048]{2,1,0:T(8,128)(2,1)S(1)}, bf16[4,16,2048]{2,1,0:T(8,128)(2,1)}, u32[]{:S(2)}) copy-start(bf16[4,16,2048]{2,1,0:T(8,128)(2,1)} %param.32) | copy-start | bytes 786436
  4.2 45.1 %copy-start.2 = (s32[16,512]{1,0:T(8,128)S(1)}, s32[16,512]{1,0:T(8,128)}, u32[]{:S(2)}) copy-start(s32[16,512]{1,0:T(8,128)} %target_v.1) | copy-start | bytes 98308
  4.2 45.1 %copy-start.3 = (bf16[4,64,128]{2,1,0:T(8,128)(2,1)S(1)}, bf16[4,64,128]{2,1,0:T(8,128)(2,1)}, u32[]{:S(2)}) copy-start(bf16[4,64,128]{2,1,0:T(8,128)(2,1)} %residual.1) | copy-start | bytes 196612
  4.2 45.1 %copy-start.4 = (s32[64]{0:T(128)S(1)}, s32[64]{0:T(128)}, u32[]{:S(2)}) copy-start(s32[64]{0:T(128)} %row_request.1) | copy-start | bytes 772
  4.2 45.1 %copy-start.5 = (s32[64]{0:T(128)S(1)}, s32[64]{0:T(128)}, u32[]{:S(2)}) copy-start(s32[64]{0:T(128)} %positions.1) | copy-start | bytes 772
  49.3 2.2 %copy-start = (bf16[2048,1024]{1,0:T(8,128)(2,1)S(1)}, bf16[2048,1024]{1,0:T(8,128)(2,1)}, u32[]{:S(2)}) copy-start(bf16[2048,1024]{1,0:T(8,128)(2,1)} %weight.1) | copy-start | bytes 12582916

commit v4 on v3

--- a/solution.py
+++ b/solution.py
@@ -391,6 +391,8 @@
         column_n = jnp.broadcast_to(found[n * 128 : (n + 1) * 128], (128, 128))
         index[n : n + 1, :] = jnp.sum(jnp.where(eye, column_n, 0), axis=0, keepdims=True)
     zero[...] = jnp.zeros_like(zero)
+    zero_out = pltpu.make_async_copy(zero, pages.at[NI * NEAR + FAR], own_sem.at[NEAR])
+    zero_out.start()
 
     def update(m, total, weighted, s, v):
         top = jnp.maximum(m, jnp.max(s, axis=1, keepdims=True))
@@ -434,6 +436,13 @@
         acc[d] = weighted
         ml[d, :, :64] = jnp.broadcast_to(m, (256, 64))
         ml[d, :, 64:] = jnp.broadcast_to(total, (256, 64))
+
+    def drain(n, c):
+        each(n, lambda c: c.wait_send())
+        for half in range(2):
+            d = n // NEAR + 2 * half
+            pltpu.make_async_copy(recv.at[d, n % NEAR], pages.at[d * NEAR + n % NEAR], page_sem.at[d, n % NEAR]).wait()
+        return c
 
     def visit(n, c):
         k = n % NEAR
@@ -463,7 +472,13 @@
             ml[d, :, 64:] = jnp.broadcast_to(total, (256, 64))
             return c
 
-        return lax.fori_loop(0, 2, request, c)
+        lax.fori_loop(0, 2, request, 0)
+
+        @pl.when(n >= NEAR)
+        def _():
+            drain(n - NEAR, 0)
+
+        return c
 
     eye = lax.broadcasted_iota(jnp.int32, (64, 128), 0) == lax.broadcasted_iota(jnp.int32, (64, 128), 1)
 
@@ -604,10 +619,19 @@
     lax.fori_loop(10, 12, visit, 0)
     parts.append(send_parts(1))
     first = reduce(0, sums[0])
+    lax.fori_loop(6, 9, drain, 0)
     sent = join(1, parts[1])
+    for copies in [zero_out, ext_out]:
+        copies.wait()
+    for copies in parts + contexts:
+        for c in copies:
+            c.wait_send()
     wide = widen(1, sent)
-    contexts += sent + wide
+    lax.fori_loop(9, 12, drain, 0)
     sums.append(project(1, wide))
+    for copies in sent + wide:
+        for c in copies:
+            c.wait_send()
     second = reduce(1, sums[1])
 
     for group in range(NI):
@@ -621,22 +645,9 @@
         for step in range(4):
             attn[step, own_rows] = ordered[step * 16 : (step + 1) * 16] + residual[step, own_rows].astype(jnp.float32)
 
-    zero_out = pltpu.make_async_copy(zero, pages.at[NI * NEAR + FAR], own_sem.at[0])
-    zero_out.start()
-    zero_out.wait()
-    ext_out.wait()
-    for copies in parts + contexts + sums:
+    for copies in sums:
         for c in copies:
             c.wait_send()
-
-    def drain(n, c):
-        each(n, lambda c: c.wait_send())
-        for half in range(2):
-            d = n // NEAR + 2 * half
-            pltpu.make_async_copy(recv.at[d, n % NEAR], pages.at[d * NEAR + n % NEAR], page_sem.at[d, n % NEAR]).wait()
-        return c
-
-    lax.fori_loop(0, 2 * NEAR, drain, 0)
 
 
 def run_main(*args):
@@ -673,7 +684,7 @@
             pltpu.VMEM((NT, 2, 64, 128), bf),
             dma((NI, NEAR, NT)),
             dma((NI, NEAR, NT)),
-            dma((NEAR,)),
+            dma((NEAR + 1,)),
             dma((NI, NEAR)),
             dma,
             dma,

time: 178 us -> 172 us (0.966)
  Pallas kernels: 170 us -> 165 us
    pallas_call x1, Pallas kernels: 122 us -> 119 us  [run_main(): pl.pallas_call(main_kernel, out_shape=(jax.ShapeDtypeStruct((NI * NEAR +...]
    pallas_call x1, Pallas kernels: 44.5 us -> 42.2 us  [move_extra(): pl.pallas_call(functools.partial(extra_kernel, p, g), out_shape=jax.Shape...]
where the time goes in v4:
time: 172 us; the launch traced here: 173 us
  Pallas kernels  165 us (96%)
  local copies, waits for them, and re-layouts  3.63 us (2%)
  other arithmetic  2.13 us (1%)
    pallas_call x1, Pallas kernels, run_main(): pl.pallas_call(main_kernel, out_shape=(jax.ShapeDtypeStruct((NI * NEAR +...  119 us
    pallas_call x1, Pallas kernels, move_extra(): pl.pallas_call(functools.partial(extra_kernel, p, g), out_shape=jax.Shape...  42.2 us
    pallas_call x1, Pallas kernels, place_pages(): pl.pallas_call(place_kernel, out_shape=jax.ShapeDtypeStruct((SLOTS, 2, 64...  4.06 us
    unnamed x14, local copies, waits for them, and re-layouts  3.63 us

profile of v4, /device:TPU:1, one launch (start us, length us, event | category | flops | bytes accessed | tf_op | source)
XLA Modules:
  0.0 172.9 jit_solution(14112676681431671964)
XLA Ops:
  0.6 0.8 add_reduce_fusion
  1.5 1.3 fusion
  3.4 0.8 copy.16
  4.2 0.0 copy-start.1
  4.2 0.0 copy-start.2
  4.2 0.0 copy-start.3
  4.2 0.0 copy-start.4
  4.2 0.0 copy-start.5
  4.2 42.6 %conditional.1 = (bf16[10,8,2,64,128]{4,3,2,1,0:T(8,128)(2,1)S(1)}) conditional(s32[]{:T(128)} %clamp.3, (s32[16]{0:T(128)}, s32[16,512]{1,0:T(8,128)}, bf16[36,2,8,64,128]{4,3,2,1,0:T(8,128)(2,1)}) %tuple.56, (s32[16]{0:T(128)}, s32[16,512]{1,0:T(8,128)}, bf16[36,2,8,64,128]{4,3,2,1,0:T(8,128)(2,1)}) %tuple.56, ...), branch_computations={%region_1.2_spmd, %region_2.3_spmd, %region_3.4_spmd, %region_4.5_... | conditional | bytes 8 | solution.py:740
  4.5 42.2 %branch_14_fun.1 = bf16[10,8,2,64,128]{4,3,2,1,0:T(8,128)(2,1)S(1)} custom-call(s32[16]{0:T(128)} %get-tuple-element.155.lengths, s32[16,512]{1,0:T(8,128)} %get-tuple-element.156.table, bf16[36,2,8,64,128]{4,3,2,1,0:T(8,128)(2,1)} %get-tuple-element.157.pool), custom_call_target="tpu_custom_call" | custom-call | tf_op jit(solution)/shard_map/cond/branch_14_fun/pallas_call | solution.py:181
  46.9 0.0 copy-done.1
  46.9 0.0 copy-done.2
  46.9 0.0 copy-done.3
  46.9 0.0 copy-done.4
  46.9 0.0 copy-done.5
  46.9 0.0 copy-start
  46.9 2.2 %copy-done = bf16[2048,1024]{1,0:T(8,128)(2,1)S(1)} copy-done((bf16[2048,1024]{1,0:T(8,128)(2,1)S(1)}, bf16[2048,1024]{1,0:T(8,128)(2,1)}, u32[]{:S(2)}) %copy-start) | copy-done | bytes 4194328
  49.1 119.1 %shard_map.113 = (bf16[35,8,2,64,128]{4,3,2,1,0:T(8,128)(2,1)S(1)}, f32[4,64,128]{2,1,0:T(8,128)S(1)}, s32[3,128]{1,0:T(4,128)S(1)}) custom-call(s32[16,512]{1,0:T(8,128)} %table.1, s32[16,512]{1,0:T(8,128)S(1)} %copy-done.2, s32[16]{0:T(128)} %lengths.1, s32[64]{0:T(128)S(1)} %copy-done.4, s32[64]{0:T(128)S(1)} %copy-done.5, ...), custom_call_target="tpu_custom_call" | custom-call | tf_op jit(solution)/shard_map/pallas_call | solution.py:656
  168.2 4.1 %shard_map.114 = bf16[288,2,64,128]{3,2,1,0:T(8,128)(2,1)} custom-call(s32[3,128]{1,0:T(4,128)S(1)} %get-tuple-element.166.index, bf16[280,2,64,128]{3,2,1,0:T(8,128)(2,1)S(1)} %bitcast.11), custom_call_target="tpu_custom_call" | custom-call | tf_op jit(solution)/shard_map/pallas_call | solution.py:716
  172.3 0.7 copy.34
Async XLA Ops:
  4.2 42.7 %copy-start.1 = (bf16[4,16,2048]{2,1,0:T(8,128)(2,1)S(1)}, bf16[4,16,2048]{2,1,0:T(8,128)(2,1)}, u32[]{:S(2)}) copy-start(bf16[4,16,2048]{2,1,0:T(8,128)(2,1)} %param.32) | copy-start | bytes 786436
  4.2 42.7 %copy-start.2 = (s32[16,512]{1,0:T(8,128)S(1)}, s32[16,512]{1,0:T(8,128)}, u32[]{:S(2)}) copy-start(s32[16,512]{1,0:T(8,128)} %target_v.1) | copy-start | bytes 98308
  4.2 42.7 %copy-start.3 = (bf16[4,64,128]{2,1,0:T(8,128)(2,1)S(1)}, bf16[4,64,128]{2,1,0:T(8,128)(2,1)}, u32[]{:S(2)}) copy-start(bf16[4,64,128]{2,1,0:T(8,128)(2,1)} %residual.1) | copy-start | bytes 196612
  4.2 42.7 %copy-start.4 = (s32[64]{0:T(128)S(1)}, s32[64]{0:T(128)}, u32[]{:S(2)}) copy-start(s32[64]{0:T(128)} %row_request.1) | copy-start | bytes 772
  4.2 42.7 %copy-start.5 = (s32[64]{0:T(128)S(1)}, s32[64]{0:T(128)}, u32[]{:S(2)}) copy-start(s32[64]{0:T(128)} %positions.1) | copy-start | bytes 772
  46.9 2.2 %copy-start = (bf16[2048,1024]{1,0:T(8,128)(2,1)S(1)}, bf16[2048,1024]{1,0:T(8,128)(2,1)}, u32[]{:S(2)}) copy-start(bf16[2048,1024]{1,0:T(8,128)(2,1)} %weight.1) | copy-start | bytes 12582916
